TPU v7x, 256 devices: a whole 4x4x8 slice. The times are simulated.
256 devices in a mesh: dom: 16 (over y_lo, z), blk: 16 (over y_hi, x, core).
Axes of the slice: x: 4, y: 4 (y_hi: 2, y_lo: 2; y = y_hi * 2 + y_lo), z: 8, core: 2. Of those that a mesh axis runs over, the one named last changes fastest.
Arguments:
- labels: bfloat16 [524288, 256], P(('dom', 'blk')), may hold values from 0.05 to 12.5
- tags: bfloat16 [524288, 256], P(('dom', 'blk')), may hold values from 0 to 2
- seed_mask: int32 [524288], P(('dom', 'blk')), may hold values 0 or 1
- intra_tiles: bfloat16 [256, 16, 2, 128, 128], P(('dom', 'blk')), may hold values from 3e-05 to 1
- intra_rows: int32 [256, 16, 2], P(('dom', 'blk')), may hold values from 0 to 15, as said below
- intra_cols: int32 [256, 16, 2], P(('dom', 'blk')), may hold values from 0 to 15
- send_list: int32 [256, 16, 1], P(('dom', 'blk')), may hold values from 0 to 15
- cut_tiles: bfloat16 [256, 16, 128, 128], P(('dom', 'blk')), may hold values from 3e-05 to 1
- cut_slot: int32 [256, 16], P(('dom', 'blk')), may hold values from 0 to 15, each once within a row
- cut_rows: int32 [256, 16], P(('dom', 'blk')), may hold values from 0 to 15, as said below
Outputs:
- new_labels: bfloat16 [524288, 256], P(('dom', 'blk'))
Inputs may be any that keep to these rules, and one draw needn't show every extreme that they name: `intra_rows`: for each device and panel the 2 entries run cyclically through the row tiles from a drawn offset, so they name distinct row tiles. `cut_slot`: each device names every slot exactly once. `cut_rows`: for each device the 16 entries run cyclically through the row tiles from a drawn offset, so every row tile has cut tiles.
All inputs are finite; a program needn't handle non-finite values. No bound on the sum of `seed_mask` on one device may be relied on, other than what follows from the above.
Results may differ from a plain program's by a relative error of at most 0.001.
Values may be sent and summed in bfloat16 or wider, within the bound.
A program may use at most 128 MiB of HBM per device.

v0:
```python
import jax
import jax.numpy as jnp
from jax import lax
from jax.sharding import PartitionSpec as P

ALPHA = 0.8


def shifted(block, axis, distance):
    devices = range(lax.axis_size(axis))
    route = [((i - distance) % len(devices), i) for i in devices]
    return lax.ppermute(block, axis, route)


def row_select(row_ids, count):
    return (row_ids[None, :] == jnp.arange(count, dtype=jnp.int32)[:, None]).astype(jnp.float32)


def aggregate(total, blocks, weights, row_ids, count):
    products = jnp.einsum("kab,kbw->kaw", weights, blocks, preferred_element_type=jnp.float32)
    return total + jnp.einsum(
        "tk,kaw->taw", row_select(row_ids, count), products, precision=lax.Precision.HIGHEST
    )


def on_device(
    labels,
    tags,
    seed_mask,
    intra_tiles,
    intra_rows,
    intra_cols,
    send_list,
    cut_tiles,
    cut_slot,
    cut_rows,
):
    weights = intra_tiles[0]
    row_ids = intra_rows[0]
    col_ids = intra_cols[0]
    sources = weights.shape[0]
    edge = weights.shape[2]
    width = labels.shape[1]
    count = labels.shape[0] // edge
    panel = labels.reshape(count, edge, width)
    empty = jnp.zeros((count, edge, width), jnp.float32)
    here = lax.axis_index("blk")

    def visit(total, current, step):
        anchor = (here - step) % sources
        picked = lax.dynamic_index_in_dim(col_ids, anchor, 0, False)
        blocks = jnp.take(current, picked, axis=0)
        return aggregate(
            total,
            blocks,
            lax.dynamic_index_in_dim(weights, anchor, 0, False),
            lax.dynamic_index_in_dim(row_ids, anchor, 0, False),
            count,
        )

    def advance(step, state):
        total, current = state
        total = visit(total, current, step)
        return (total, shifted(current, "blk", 1))

    total, current = lax.fori_loop(0, sources - 1, advance, (empty, panel))
    total = visit(total, current, sources - 1)
    lists = send_list[0]
    domains = lists.shape[0]
    copies = lists.shape[1]
    slot_ids = cut_slot[0]
    outgoing = jnp.take(panel, lists.reshape(-1), axis=0).reshape(domains, copies, edge, width)
    arrived = lax.all_to_all(outgoing, "dom", split_axis=0, concat_axis=0, tiled=True).reshape(
        domains * copies, edge, width
    )
    cut_blocks = jnp.take(arrived, slot_ids, axis=0)
    total = aggregate(total, cut_blocks, cut_tiles[0], cut_rows[0], count)
    unit = jnp.ones((edge,), jnp.bfloat16)
    inner = jnp.einsum("skab,b->ska", weights, unit, preferred_element_type=jnp.float32).reshape(
        -1, edge
    )
    outer = jnp.einsum("kab,b->ka", cut_tiles[0], unit, preferred_element_type=jnp.float32)
    degree = jnp.dot(row_select(row_ids.reshape(-1), count), inner, precision=lax.Precision.HIGHEST)
    degree = degree + jnp.dot(
        row_select(cut_rows[0], count), outer, precision=lax.Precision.HIGHEST
    )
    prior = tags.reshape(count, edge, width).astype(jnp.float32)
    seeded = seed_mask.reshape(count, edge, 1)
    mixed = ALPHA * total / degree[:, :, None] + (1.0 - ALPHA) * prior
    return jnp.where(seeded == 1, prior, mixed).astype(jnp.bfloat16).reshape(count * edge, width)


def solution(mesh):
    placed = (
        P(("dom", "blk"), None),
        P(("dom", "blk"), None),
        P(("dom", "blk")),
        P(("dom", "blk"), None, None, None, None),
        P(("dom", "blk"), None, None),
        P(("dom", "blk"), None, None),
        P(("dom", "blk"), None, None),
        P(("dom", "blk"), None, None, None),
        P(("dom", "blk"), None),
        P(("dom", "blk"), None),
    )
    return jax.shard_map(
        on_device, mesh=mesh, in_specs=placed, out_specs=P(("dom", "blk"), None), check_vma=False
    )
```

profile of v0, /device:TPU:32, one launch (start us, length us, event | category | flops | bytes accessed | tf_op | source)
XLA Modules:
  0.0 313.5 jit_solution(8644676501854369018)
XLA Ops:
  0.0 1.3 copy.54
  1.3 0.6 gather_fusion.2
  2.0 1.1 select_bitcast_fusion
  3.1 9.7 %all-to-all-start = ((bf16[16,1,128,256]{3,2,1,0:T(8,128)(2,1)}), bf16[16,1,128,256]{3,2,1,0:T(8,128)(2,1)}, u32[]{:S(2)}, u32[]{:S(2)}) async-start(bf16[16,1,128,256]{3,2,1,0:T(8,128)(2,1)} %select_bitcast_fusion), calls=%async_computation | async-start | bytes 2097152 | tf_op jit(solution)/shard_map/all_to_all | solution.py:73
  13.4 1.6 fusion.41
  15.7 1.6 convert.1
  17.4 277.5 %while.18 = (s32[]{:T(128)}, f32[16,128,256]{2,0,1:T(8,128)}, bf16[16,128,256]{2,1,0:T(8,128)(2,1)S(1)}, s32[]{:T(128)}, s32[16,2]{1,0:T(8,128)S(1)}, /*index=5*...) while((s32[]{:T(128)}, f32[16,128,256]{2,0,1:T(8,128)}, ...), condition=%wide.region_1.3_spmd.clone, body=%wide.region_0.2_spmd.clone.sunk | while | flops 30475324 | bytes 11473282 | solution.py:66
  17.6 0.6 gather_fusion
  18.2 1.1 fusion.61
  19.3 2.6 select_add_fusion.2
  21.9 21.1 %collective-permute-done = bf16[16,128,256]{2,1,0:T(8,128)(2,1)S(1)} collective-permute-done((bf16[16,128,256]{2,1,0:T(8,128)(2,1)S(1)}, bf16[16,128,256]{2,1,0:T(8,128)(2,1)S(1)}, u32[]{:S(2)}, u32[]{:S(2)}) %collective-permute-start) | collective-permute-done | bytes 1048608 | tf_op jit(solution)/shard_map/while/body/eval_jaxpr/ppermute | solution.py:12
  43.3 0.6 gather_fusion
  43.8 1.1 fusion.61
  44.9 3.8 %select_add_fusion.2 = f32[16,128,256]{2,0,1:T(8,128)} fusion(f32[16,128,256]{2,0,1:T(8,128)} %get-tuple-element.309, pred[]{:T(512)S(6)} %compare.5, f32[2,128,256]{2,1,0:T(8,128)S(1)} %fusion.61, s32[2]{0:T(128)S(1)} %fusion.62), kind=kOutput, calls=%fused_computation.4.clone.1 | convolution fusion | flops 13631520 | bytes 4456457 | tf_op jit(solution)/shard_map/while/body/eval_jaxpr/tk,kaw->taw/dot_general | solution.py:21
  48.7 12.3 %collective-permute-done = bf16[16,128,256]{2,1,0:T(8,128)(2,1)S(1)} collective-permute-done((bf16[16,128,256]{2,1,0:T(8,128)(2,1)S(1)}, bf16[16,128,256]{2,1,0:T(8,128)(2,1)S(1)}, u32[]{:S(2)}, u32[]{:S(2)}) %collective-permute-start) | collective-permute-done | bytes 1048608 | tf_op jit(solution)/shard_map/while/body/eval_jaxpr/ppermute | solution.py:12
  61.3 0.6 gather_fusion
  61.8 1.1 fusion.61
  62.9 3.8 %select_add_fusion.2 = f32[16,128,256]{2,0,1:T(8,128)} fusion(f32[16,128,256]{2,0,1:T(8,128)} %get-tuple-element.309, pred[]{:T(512)S(6)} %compare.5, f32[2,128,256]{2,1,0:T(8,128)S(1)} %fusion.61, s32[2]{0:T(128)S(1)} %fusion.62), kind=kOutput, calls=%fused_computation.4.clone.1 | convolution fusion | flops 13631520 | bytes 4456457 | tf_op jit(solution)/shard_map/while/body/eval_jaxpr/tk,kaw->taw/dot_general | solution.py:21
  66.7 12.3 %collective-permute-done = bf16[16,128,256]{2,1,0:T(8,128)(2,1)S(1)} collective-permute-done((bf16[16,128,256]{2,1,0:T(8,128)(2,1)S(1)}, bf16[16,128,256]{2,1,0:T(8,128)(2,1)S(1)}, u32[]{:S(2)}, u32[]{:S(2)}) %collective-permute-start) | collective-permute-done | bytes 1048608 | tf_op jit(solution)/shard_map/while/body/eval_jaxpr/ppermute | solution.py:12
  79.2 0.6 gather_fusion
  79.8 1.1 fusion.61
  80.9 3.8 %select_add_fusion.2 = f32[16,128,256]{2,0,1:T(8,128)} fusion(f32[16,128,256]{2,0,1:T(8,128)} %get-tuple-element.309, pred[]{:T(512)S(6)} %compare.5, f32[2,128,256]{2,1,0:T(8,128)S(1)} %fusion.61, s32[2]{0:T(128)S(1)} %fusion.62), kind=kOutput, calls=%fused_computation.4.clone.1 | convolution fusion | flops 13631520 | bytes 4456457 | tf_op jit(solution)/shard_map/while/body/eval_jaxpr/tk,kaw->taw/dot_general | solution.py:21
  84.7 12.3 %collective-permute-done = bf16[16,128,256]{2,1,0:T(8,128)(2,1)S(1)} collective-permute-done((bf16[16,128,256]{2,1,0:T(8,128)(2,1)S(1)}, bf16[16,128,256]{2,1,0:T(8,128)(2,1)S(1)}, u32[]{:S(2)}, u32[]{:S(2)}) %collective-permute-start) | collective-permute-done | bytes 1048608 | tf_op jit(solution)/shard_map/while/body/eval_jaxpr/ppermute | solution.py:12
  97.8 1.1 fusion.61
  98.9 3.8 %select_add_fusion.2 = f32[16,128,256]{2,0,1:T(8,128)} fusion(f32[16,128,256]{2,0,1:T(8,128)} %get-tuple-element.309, pred[]{:T(512)S(6)} %compare.5, f32[2,128,256]{2,1,0:T(8,128)S(1)} %fusion.61, s32[2]{0:T(128)S(1)} %fusion.62), kind=kOutput, calls=%fused_computation.4.clone.1 | convolution fusion | flops 13631520 | bytes 4456457 | tf_op jit(solution)/shard_map/while/body/eval_jaxpr/tk,kaw->taw/dot_general | solution.py:21
  102.7 12.3 %collective-permute-done = bf16[16,128,256]{2,1,0:T(8,128)(2,1)S(1)} collective-permute-done((bf16[16,128,256]{2,1,0:T(8,128)(2,1)S(1)}, bf16[16,128,256]{2,1,0:T(8,128)(2,1)S(1)}, u32[]{:S(2)}, u32[]{:S(2)}) %collective-permute-start) | collective-permute-done | bytes 1048608 | tf_op jit(solution)/shard_map/while/body/eval_jaxpr/ppermute | solution.py:12
  115.2 0.6 gather_fusion
  115.8 1.1 fusion.61
  116.9 3.8 %select_add_fusion.2 = f32[16,128,256]{2,0,1:T(8,128)} fusion(f32[16,128,256]{2,0,1:T(8,128)} %get-tuple-element.309, pred[]{:T(512)S(6)} %compare.5, f32[2,128,256]{2,1,0:T(8,128)S(1)} %fusion.61, s32[2]{0:T(128)S(1)} %fusion.62), kind=kOutput, calls=%fused_computation.4.clone.1 | convolution fusion | flops 13631520 | bytes 4456457 | tf_op jit(solution)/shard_map/while/body/eval_jaxpr/tk,kaw->taw/dot_general | solution.py:21
  120.7 12.3 %collective-permute-done = bf16[16,128,256]{2,1,0:T(8,128)(2,1)S(1)} collective-permute-done((bf16[16,128,256]{2,1,0:T(8,128)(2,1)S(1)}, bf16[16,128,256]{2,1,0:T(8,128)(2,1)S(1)}, u32[]{:S(2)}, u32[]{:S(2)}) %collective-permute-start) | collective-permute-done | bytes 1048608 | tf_op jit(solution)/shard_map/while/body/eval_jaxpr/ppermute | solution.py:12
  133.8 1.1 fusion.61
  134.9 3.8 %select_add_fusion.2 = f32[16,128,256]{2,0,1:T(8,128)} fusion(f32[16,128,256]{2,0,1:T(8,128)} %get-tuple-element.309, pred[]{:T(512)S(6)} %compare.5, f32[2,128,256]{2,1,0:T(8,128)S(1)} %fusion.61, s32[2]{0:T(128)S(1)} %fusion.62), kind=kOutput, calls=%fused_computation.4.clone.1 | convolution fusion | flops 13631520 | bytes 4456457 | tf_op jit(solution)/shard_map/while/body/eval_jaxpr/tk,kaw->taw/dot_general | solution.py:21
  138.7 12.3 %collective-permute-done = bf16[16,128,256]{2,1,0:T(8,128)(2,1)S(1)} collective-permute-done((bf16[16,128,256]{2,1,0:T(8,128)(2,1)S(1)}, bf16[16,128,256]{2,1,0:T(8,128)(2,1)S(1)}, u32[]{:S(2)}, u32[]{:S(2)}) %collective-permute-start) | collective-permute-done | bytes 1048608 | tf_op jit(solution)/shard_map/while/body/eval_jaxpr/ppermute | solution.py:12
  151.8 1.1 fusion.61
  152.9 3.8 %select_add_fusion.2 = f32[16,128,256]{2,0,1:T(8,128)} fusion(f32[16,128,256]{2,0,1:T(8,128)} %get-tuple-element.309, pred[]{:T(512)S(6)} %compare.5, f32[2,128,256]{2,1,0:T(8,128)S(1)} %fusion.61, s32[2]{0:T(128)S(1)} %fusion.62), kind=kOutput, calls=%fused_computation.4.clone.1 | convolution fusion | flops 13631520 | bytes 4456457 | tf_op jit(solution)/shard_map/while/body/eval_jaxpr/tk,kaw->taw/dot_general | solution.py:21
  156.6 12.3 %collective-permute-done = bf16[16,128,256]{2,1,0:T(8,128)(2,1)S(1)} collective-permute-done((bf16[16,128,256]{2,1,0:T(8,128)(2,1)S(1)}, bf16[16,128,256]{2,1,0:T(8,128)(2,1)S(1)}, u32[]{:S(2)}, u32[]{:S(2)}) %collective-permute-start) | collective-permute-done | bytes 1048608 | tf_op jit(solution)/shard_map/while/body/eval_jaxpr/ppermute | solution.py:12
  169.8 1.1 fusion.61
  170.9 3.8 %select_add_fusion.2 = f32[16,128,256]{2,0,1:T(8,128)} fusion(f32[16,128,256]{2,0,1:T(8,128)} %get-tuple-element.309, pred[]{:T(512)S(6)} %compare.5, f32[2,128,256]{2,1,0:T(8,128)S(1)} %fusion.61, s32[2]{0:T(128)S(1)} %fusion.62), kind=kOutput, calls=%fused_computation.4.clone.1 | convolution fusion | flops 13631520 | bytes 4456457 | tf_op jit(solution)/shard_map/while/body/eval_jaxpr/tk,kaw->taw/dot_general | solution.py:21
  174.6 12.3 %collective-permute-done = bf16[16,128,256]{2,1,0:T(8,128)(2,1)S(1)} collective-permute-done((bf16[16,128,256]{2,1,0:T(8,128)(2,1)S(1)}, bf16[16,128,256]{2,1,0:T(8,128)(2,1)S(1)}, u32[]{:S(2)}, u32[]{:S(2)}) %collective-permute-start) | collective-permute-done | bytes 1048608 | tf_op jit(solution)/shard_map/while/body/eval_jaxpr/ppermute | solution.py:12
  187.8 1.1 fusion.61
  188.9 3.8 %select_add_fusion.2 = f32[16,128,256]{2,0,1:T(8,128)} fusion(f32[16,128,256]{2,0,1:T(8,128)} %get-tuple-element.309, pred[]{:T(512)S(6)} %compare.5, f32[2,128,256]{2,1,0:T(8,128)S(1)} %fusion.61, s32[2]{0:T(128)S(1)} %fusion.62), kind=kOutput, calls=%fused_computation.4.clone.1 | convolution fusion | flops 13631520 | bytes 4456457 | tf_op jit(solution)/shard_map/while/body/eval_jaxpr/tk,kaw->taw/dot_general | solution.py:21
  192.6 12.3 %collective-permute-done = bf16[16,128,256]{2,1,0:T(8,128)(2,1)S(1)} collective-permute-done((bf16[16,128,256]{2,1,0:T(8,128)(2,1)S(1)}, bf16[16,128,256]{2,1,0:T(8,128)(2,1)S(1)}, u32[]{:S(2)}, u32[]{:S(2)}) %collective-permute-start) | collective-permute-done | bytes 1048608 | tf_op jit(solution)/shard_map/while/body/eval_jaxpr/ppermute | solution.py:12
  205.8 1.1 fusion.61
  206.9 3.8 %select_add_fusion.2 = f32[16,128,256]{2,0,1:T(8,128)} fusion(f32[16,128,256]{2,0,1:T(8,128)} %get-tuple-element.309, pred[]{:T(512)S(6)} %compare.5, f32[2,128,256]{2,1,0:T(8,128)S(1)} %fusion.61, s32[2]{0:T(128)S(1)} %fusion.62), kind=kOutput, calls=%fused_computation.4.clone.1 | convolution fusion | flops 13631520 | bytes 4456457 | tf_op jit(solution)/shard_map/while/body/eval_jaxpr/tk,kaw->taw/dot_general | solution.py:21
  210.6 12.3 %collective-permute-done = bf16[16,128,256]{2,1,0:T(8,128)(2,1)S(1)} collective-permute-done((bf16[16,128,256]{2,1,0:T(8,128)(2,1)S(1)}, bf16[16,128,256]{2,1,0:T(8,128)(2,1)S(1)}, u32[]{:S(2)}, u32[]{:S(2)}) %collective-permute-start) | collective-permute-done | bytes 1048608 | tf_op jit(solution)/shard_map/while/body/eval_jaxpr/ppermute | solution.py:12
  223.8 1.1 fusion.61
  224.8 3.8 %select_add_fusion.2 = f32[16,128,256]{2,0,1:T(8,128)} fusion(f32[16,128,256]{2,0,1:T(8,128)} %get-tuple-element.309, pred[]{:T(512)S(6)} %compare.5, f32[2,128,256]{2,1,0:T(8,128)S(1)} %fusion.61, s32[2]{0:T(128)S(1)} %fusion.62), kind=kOutput, calls=%fused_computation.4.clone.1 | convolution fusion | flops 13631520 | bytes 4456457 | tf_op jit(solution)/shard_map/while/body/eval_jaxpr/tk,kaw->taw/dot_general | solution.py:21
  228.6 12.3 %collective-permute-done = bf16[16,128,256]{2,1,0:T(8,128)(2,1)S(1)} collective-permute-done((bf16[16,128,256]{2,1,0:T(8,128)(2,1)S(1)}, bf16[16,128,256]{2,1,0:T(8,128)(2,1)S(1)}, u32[]{:S(2)}, u32[]{:S(2)}) %collective-permute-start) | collective-permute-done | bytes 1048608 | tf_op jit(solution)/shard_map/while/body/eval_jaxpr/ppermute | solution.py:12
  241.7 1.1 fusion.61
  242.8 3.8 %select_add_fusion.2 = f32[16,128,256]{2,0,1:T(8,128)} fusion(f32[16,128,256]{2,0,1:T(8,128)} %get-tuple-element.309, pred[]{:T(512)S(6)} %compare.5, f32[2,128,256]{2,1,0:T(8,128)S(1)} %fusion.61, s32[2]{0:T(128)S(1)} %fusion.62), kind=kOutput, calls=%fused_computation.4.clone.1 | convolution fusion | flops 13631520 | bytes 4456457 | tf_op jit(solution)/shard_map/while/body/eval_jaxpr/tk,kaw->taw/dot_general | solution.py:21
  246.6 12.3 %collective-permute-done = bf16[16,128,256]{2,1,0:T(8,128)(2,1)S(1)} collective-permute-done((bf16[16,128,256]{2,1,0:T(8,128)(2,1)S(1)}, bf16[16,128,256]{2,1,0:T(8,128)(2,1)S(1)}, u32[]{:S(2)}, u32[]{:S(2)}) %collective-permute-start) | collective-permute-done | bytes 1048608 | tf_op jit(solution)/shard_map/while/body/eval_jaxpr/ppermute | solution.py:12
  259.7 1.1 fusion.61
  260.8 3.8 %select_add_fusion.2 = f32[16,128,256]{2,0,1:T(8,128)} fusion(f32[16,128,256]{2,0,1:T(8,128)} %get-tuple-element.309, pred[]{:T(512)S(6)} %compare.5, f32[2,128,256]{2,1,0:T(8,128)S(1)} %fusion.61, s32[2]{0:T(128)S(1)} %fusion.62), kind=kOutput, calls=%fused_computation.4.clone.1 | convolution fusion | flops 13631520 | bytes 4456457 | tf_op jit(solution)/shard_map/while/body/eval_jaxpr/tk,kaw->taw/dot_general | solution.py:21
  264.6 12.3 %collective-permute-done = bf16[16,128,256]{2,1,0:T(8,128)(2,1)S(1)} collective-permute-done((bf16[16,128,256]{2,1,0:T(8,128)(2,1)S(1)}, bf16[16,128,256]{2,1,0:T(8,128)(2,1)S(1)}, u32[]{:S(2)}, u32[]{:S(2)}) %collective-permute-start) | collective-permute-done | bytes 1048608 | tf_op jit(solution)/shard_map/while/body/eval_jaxpr/ppermute | solution.py:12
  277.7 1.1 fusion.61
  278.8 3.8 %select_add_fusion.2 = f32[16,128,256]{2,0,1:T(8,128)} fusion(f32[16,128,256]{2,0,1:T(8,128)} %get-tuple-element.309, pred[]{:T(512)S(6)} %compare.5, f32[2,128,256]{2,1,0:T(8,128)S(1)} %fusion.61, s32[2]{0:T(128)S(1)} %fusion.62), kind=kOutput, calls=%fused_computation.4.clone.1 | convolution fusion | flops 13631520 | bytes 4456457 | tf_op jit(solution)/shard_map/while/body/eval_jaxpr/tk,kaw->taw/dot_general | solution.py:21
  282.6 12.3 %collective-permute-done = bf16[16,128,256]{2,1,0:T(8,128)(2,1)S(1)} collective-permute-done((bf16[16,128,256]{2,1,0:T(8,128)(2,1)S(1)}, bf16[16,128,256]{2,1,0:T(8,128)(2,1)S(1)}, u32[]{:S(2)}, u32[]{:S(2)}) %collective-permute-start) | collective-permute-done | bytes 1048608 | tf_op jit(solution)/shard_map/while/body/eval_jaxpr/ppermute | solution.py:12
  295.5 1.1 fusion.23
  296.6 2.5 fusion.21
  299.1 1.8 gather_fusion.3
  301.0 1.9 convolution_bitcast_fusion
  302.9 3.1 copy.29
  306.0 6.2 %select_convert_fusion = bf16[16,128,256]{2,0,1:T(8,128)(2,1)S(1)} fusion(f32[16,128,256]{2,1,0:T(8,128)} %convert.1, f32[16,128,256]{2,0,1:T(8,128)} %get-tuple-element.185, f32[16,128,256]{2,0,1:T(8,128)} %fusion.21, f32[16,128,256]{2,0,1:T(8,128)} %copy.29, f32[16,128]{0,1:T(8,128)S(1)} %copy.31, pred[16,128]{0,1:T(8,128)(4,1)S(1)} %copy.24, ...), kind=kOutput, calls=%fused_computation.25 | convolution fusion | flops 104857856 | bytes 9447488 | tf_op jit(solution)/shard_map/tk,kaw->taw/dot_general | solution.py:21
  312.2 1.3 copy.34
  (124 shorter events, 10.3 us)
Async XLA Ops:
  0.0 15.1 %copy-start = (bf16[1,16,128,128]{3,2,1,0:T(8,128)(2,1)S(1)}, bf16[1,16,128,128]{3,2,1,0:T(8,128)(2,1)}, u32[]{:S(2)}) copy-start(bf16[1,16,128,128]{3,2,1,0:T(8,128)(2,1)} %param.23) | copy-start | bytes 1572868
  0.0 1.3 copy-start.6
  2.0 10.9 %copy-start.2 = (s32[1,16,2]{1,2,0:T(2,128)S(1)}, s32[1,16,2]{1,2,0:T(2,128)}, u32[]{:S(2)}) copy-start(s32[1,16,2]{1,2,0:T(2,128)} %param.20) | copy-start | bytes 388
  2.0 11.0 %copy-start.4 = (s32[1,16,2]{1,2,0:T(2,128)S(1)}, s32[1,16,2]{1,2,0:T(2,128)}, u32[]{:S(2)}) copy-start(s32[1,16,2]{1,2,0:T(2,128)} %param.21) | copy-start | bytes 388
  3.1 12.3 %copy-start.5 = (s32[1,16]{1,0:T(1,128)S(1)}, s32[1,16]{1,0:T(1,128)}, u32[]{:S(2)}) copy-start(s32[1,16]{1,0:T(1,128)} %param.25) | copy-start | bytes 196
  3.1 12.6 %copy-start.1 = (bf16[2048,256]{1,0:T(8,128)(2,1)S(1)}, bf16[2048,256]{1,0:T(8,128)(2,1)}, u32[]{:S(2)}) copy-start(bf16[2048,256]{1,0:T(8,128)(2,1)} %param.17) | copy-start | bytes 3145732
  3.1 296.0 %all-to-all-start = ((bf16[16,1,128,256]{3,2,1,0:T(8,128)(2,1)}), bf16[16,1,128,256]{3,2,1,0:T(8,128)(2,1)}, u32[]{:S(2)}, u32[]{:S(2)}) async-start(bf16[16,1,128,256]{3,2,1,0:T(8,128)(2,1)} %select_bitcast_fusion), calls=%async_computation | async-start | bytes 2097152 | tf_op jit(solution)/shard_map/all_to_all | solution.py:73
  14.9 2.3 copy-start.3
  17.4 278.1 %copy-start.7 = (s32[1,16]{1,0:T(1,128)S(1)}, s32[1,16]{1,0:T(1,128)}, u32[]{:S(2)}) copy-start(s32[1,16]{1,0:T(1,128)} %param.24) | copy-start | bytes 196
  17.5 25.5 %collective-permute-start = (bf16[16,128,256]{2,1,0:T(8,128)(2,1)S(1)}, bf16[16,128,256]{2,1,0:T(8,128)(2,1)S(1)}, u32[]{:S(2)}, u32[]{:S(2)}) collective-permute-start(bf16[16,128,256]{2,1,0:T(8,128)(2,1)S(1)} %copy.50), channel_id=1, source_target_pairs={{15,0},{0,1},{1,2},{2,3},{3,4},{4,5},{5,6},{6,7},{7,8},{8,9},{9,10... | collective-permute-start | bytes 3145736 | tf_op jit(solution)/shard_map/while/body/eval_jaxpr/ppermute | solution.py:12
  43.1 17.9 %collective-permute-start = (bf16[16,128,256]{2,1,0:T(8,128)(2,1)S(1)}, bf16[16,128,256]{2,1,0:T(8,128)(2,1)S(1)}, u32[]{:S(2)}, u32[]{:S(2)}) collective-permute-start(bf16[16,128,256]{2,1,0:T(8,128)(2,1)S(1)} %copy.50), channel_id=1, source_target_pairs={{15,0},{0,1},{1,2},{2,3},{3,4},{4,5},{5,6},{6,7},{7,8},{8,9},{9,10... | collective-permute-start | bytes 3145736 | tf_op jit(solution)/shard_map/while/body/eval_jaxpr/ppermute | solution.py:12
  61.1 17.9 %collective-permute-start = (bf16[16,128,256]{2,1,0:T(8,128)(2,1)S(1)}, bf16[16,128,256]{2,1,0:T(8,128)(2,1)S(1)}, u32[]{:S(2)}, u32[]{:S(2)}) collective-permute-start(bf16[16,128,256]{2,1,0:T(8,128)(2,1)S(1)} %copy.50), channel_id=1, source_target_pairs={{15,0},{0,1},{1,2},{2,3},{3,4},{4,5},{5,6},{6,7},{7,8},{8,9},{9,10... | collective-permute-start | bytes 3145736 | tf_op jit(solution)/shard_map/while/body/eval_jaxpr/ppermute | solution.py:12
  79.1 17.9 %collective-permute-start = (bf16[16,128,256]{2,1,0:T(8,128)(2,1)S(1)}, bf16[16,128,256]{2,1,0:T(8,128)(2,1)S(1)}, u32[]{:S(2)}, u32[]{:S(2)}) collective-permute-start(bf16[16,128,256]{2,1,0:T(8,128)(2,1)S(1)} %copy.50), channel_id=1, source_target_pairs={{15,0},{0,1},{1,2},{2,3},{3,4},{4,5},{5,6},{6,7},{7,8},{8,9},{9,10... | collective-permute-start | bytes 3145736 | tf_op jit(solution)/shard_map/while/body/eval_jaxpr/ppermute | solution.py:12
  97.1 17.9 %collective-permute-start = (bf16[16,128,256]{2,1,0:T(8,128)(2,1)S(1)}, bf16[16,128,256]{2,1,0:T(8,128)(2,1)S(1)}, u32[]{:S(2)}, u32[]{:S(2)}) collective-permute-start(bf16[16,128,256]{2,1,0:T(8,128)(2,1)S(1)} %copy.50), channel_id=1, source_target_pairs={{15,0},{0,1},{1,2},{2,3},{3,4},{4,5},{5,6},{6,7},{7,8},{8,9},{9,10... | collective-permute-start | bytes 3145736 | tf_op jit(solution)/shard_map/while/body/eval_jaxpr/ppermute | solution.py:12
  115.1 17.9 %collective-permute-start = (bf16[16,128,256]{2,1,0:T(8,128)(2,1)S(1)}, bf16[16,128,256]{2,1,0:T(8,128)(2,1)S(1)}, u32[]{:S(2)}, u32[]{:S(2)}) collective-permute-start(bf16[16,128,256]{2,1,0:T(8,128)(2,1)S(1)} %copy.50), channel_id=1, source_target_pairs={{15,0},{0,1},{1,2},{2,3},{3,4},{4,5},{5,6},{6,7},{7,8},{8,9},{9,10... | collective-permute-start | bytes 3145736 | tf_op jit(solution)/shard_map/while/body/eval_jaxpr/ppermute | solution.py:12
  133.1 17.9 %collective-permute-start = (bf16[16,128,256]{2,1,0:T(8,128)(2,1)S(1)}, bf16[16,128,256]{2,1,0:T(8,128)(2,1)S(1)}, u32[]{:S(2)}, u32[]{:S(2)}) collective-permute-start(bf16[16,128,256]{2,1,0:T(8,128)(2,1)S(1)} %copy.50), channel_id=1, source_target_pairs={{15,0},{0,1},{1,2},{2,3},{3,4},{4,5},{5,6},{6,7},{7,8},{8,9},{9,10... | collective-permute-start | bytes 3145736 | tf_op jit(solution)/shard_map/while/body/eval_jaxpr/ppermute | solution.py:12
  151.1 17.9 %collective-permute-start = (bf16[16,128,256]{2,1,0:T(8,128)(2,1)S(1)}, bf16[16,128,256]{2,1,0:T(8,128)(2,1)S(1)}, u32[]{:S(2)}, u32[]{:S(2)}) collective-permute-start(bf16[16,128,256]{2,1,0:T(8,128)(2,1)S(1)} %copy.50), channel_id=1, source_target_pairs={{15,0},{0,1},{1,2},{2,3},{3,4},{4,5},{5,6},{6,7},{7,8},{8,9},{9,10... | collective-permute-start | bytes 3145736 | tf_op jit(solution)/shard_map/while/body/eval_jaxpr/ppermute | solution.py:12
  169.0 17.9 %collective-permute-start = (bf16[16,128,256]{2,1,0:T(8,128)(2,1)S(1)}, bf16[16,128,256]{2,1,0:T(8,128)(2,1)S(1)}, u32[]{:S(2)}, u32[]{:S(2)}) collective-permute-start(bf16[16,128,256]{2,1,0:T(8,128)(2,1)S(1)} %copy.50), channel_id=1, source_target_pairs={{15,0},{0,1},{1,2},{2,3},{3,4},{4,5},{5,6},{6,7},{7,8},{8,9},{9,10... | collective-permute-start | bytes 3145736 | tf_op jit(solution)/shard_map/while/body/eval_jaxpr/ppermute | solution.py:12
  187.0 17.9 %collective-permute-start = (bf16[16,128,256]{2,1,0:T(8,128)(2,1)S(1)}, bf16[16,128,256]{2,1,0:T(8,128)(2,1)S(1)}, u32[]{:S(2)}, u32[]{:S(2)}) collective-permute-start(bf16[16,128,256]{2,1,0:T(8,128)(2,1)S(1)} %copy.50), channel_id=1, source_target_pairs={{15,0},{0,1},{1,2},{2,3},{3,4},{4,5},{5,6},{6,7},{7,8},{8,9},{9,10... | collective-permute-start | bytes 3145736 | tf_op jit(solution)/shard_map/while/body/eval_jaxpr/ppermute | solution.py:12
  205.0 17.9 %collective-permute-start = (bf16[16,128,256]{2,1,0:T(8,128)(2,1)S(1)}, bf16[16,128,256]{2,1,0:T(8,128)(2,1)S(1)}, u32[]{:S(2)}, u32[]{:S(2)}) collective-permute-start(bf16[16,128,256]{2,1,0:T(8,128)(2,1)S(1)} %copy.50), channel_id=1, source_target_pairs={{15,0},{0,1},{1,2},{2,3},{3,4},{4,5},{5,6},{6,7},{7,8},{8,9},{9,10... | collective-permute-start | bytes 3145736 | tf_op jit(solution)/shard_map/while/body/eval_jaxpr/ppermute | solution.py:12
  223.0 17.9 %collective-permute-start = (bf16[16,128,256]{2,1,0:T(8,128)(2,1)S(1)}, bf16[16,128,256]{2,1,0:T(8,128)(2,1)S(1)}, u32[]{:S(2)}, u32[]{:S(2)}) collective-permute-start(bf16[16,128,256]{2,1,0:T(8,128)(2,1)S(1)} %copy.50), channel_id=1, source_target_pairs={{15,0},{0,1},{1,2},{2,3},{3,4},{4,5},{5,6},{6,7},{7,8},{8,9},{9,10... | collective-permute-start | bytes 3145736 | tf_op jit(solution)/shard_map/while/body/eval_jaxpr/ppermute | solution.py:12
  241.0 17.9 %collective-permute-start = (bf16[16,128,256]{2,1,0:T(8,128)(2,1)S(1)}, bf16[16,128,256]{2,1,0:T(8,128)(2,1)S(1)}, u32[]{:S(2)}, u32[]{:S(2)}) collective-permute-start(bf16[16,128,256]{2,1,0:T(8,128)(2,1)S(1)} %copy.50), channel_id=1, source_target_pairs={{15,0},{0,1},{1,2},{2,3},{3,4},{4,5},{5,6},{6,7},{7,8},{8,9},{9,10... | collective-permute-start | bytes 3145736 | tf_op jit(solution)/shard_map/while/body/eval_jaxpr/ppermute | solution.py:12
  259.0 17.9 %collective-permute-start = (bf16[16,128,256]{2,1,0:T(8,128)(2,1)S(1)}, bf16[16,128,256]{2,1,0:T(8,128)(2,1)S(1)}, u32[]{:S(2)}, u32[]{:S(2)}) collective-permute-start(bf16[16,128,256]{2,1,0:T(8,128)(2,1)S(1)} %copy.50), channel_id=1, source_target_pairs={{15,0},{0,1},{1,2},{2,3},{3,4},{4,5},{5,6},{6,7},{7,8},{8,9},{9,10... | collective-permute-start | bytes 3145736 | tf_op jit(solution)/shard_map/while/body/eval_jaxpr/ppermute | solution.py:12
  277.0 17.9 %collective-permute-start = (bf16[16,128,256]{2,1,0:T(8,128)(2,1)S(1)}, bf16[16,128,256]{2,1,0:T(8,128)(2,1)S(1)}, u32[]{:S(2)}, u32[]{:S(2)}) collective-permute-start(bf16[16,128,256]{2,1,0:T(8,128)(2,1)S(1)} %copy.50), channel_id=1, source_target_pairs={{15,0},{0,1},{1,2},{2,3},{3,4},{4,5},{5,6},{6,7},{7,8},{8,9},{9,10... | collective-permute-start | bytes 3145736 | tf_op jit(solution)/shard_map/while/body/eval_jaxpr/ppermute | solution.py:12
where the time goes:
time: 315 us; the launch traced here: 314 us
  waiting for transfers between devices  194 us (62%)
  matrix products  85.3 us (27%)
  local copies, waits for them, and re-layouts  19.1 us (6%)
  starting transfers between devices  11 us (3%)
    ppermute x15, waiting for transfers between devices, shifted(): return lax.ppermute(block, axis, route)  194 us
    dot_general x17, matrix products, aggregate(): jnp.einsum('tk,kaw->taw', row_select(row_ids, count), products, precision...  63.9 us
    dot_general x17, matrix products, aggregate(): jnp.einsum('kab,kbw->kaw', weights, blocks, preferred_element_type=jnp.fl...  19.3 us
    all_to_all x1, starting transfers between devices, on_device(): lax.all_to_all(outgoing, 'dom', split_axis=0, concat_axis=0, tiled=True)  9.73 us
    gather x16, local copies, waits for them, and re-layouts, visit(): blocks = jnp.take(current, picked, axis=0)  8.88 us
  transfers between devices with their start and end apart: 16, of which 15 were waited for; matrix products, arithmetic and copies ran while one was open for 29% of the time, Pallas kernels for 0%

commit v1 on v0

v1 whole, which is shorter than its diff:
```python
import functools

import jax
import jax.numpy as jnp
from jax import lax
from jax.experimental import pallas as pl
from jax.experimental.pallas import tpu as pltpu
from jax.sharding import PartitionSpec as P

ALPHA = 0.8
MESH = pl.DeviceIdType.MESH
F32 = jnp.float32
BF16 = jnp.bfloat16
I32 = jnp.int32
TILES = 16
EDGE = 128
WIDTH = 256
GRAIN = 16
GROUP = 8
CHUNKS = (1, 1, 1, 1, 1, 1, 1, 1)
WINDOW = 3


def kernel(
    labels,
    tags,
    seeds,
    intra,
    cut,
    rows_hbm,
    cols_hbm,
    list_hbm,
    slot_hbm,
    crow_hbm,
    out,
    panel,
    prior,
    seedv,
    wi,
    wc,
    irows,
    icols,
    slist,
    cslot,
    crows,
    colmsg,
    listmsg,
    request_land,
    list_land,
    requests,
    partner_list,
    inverse,
    partner_parts,
    mirror_parts,
    x_stage_own,
    x_recv_own,
    x_stage,
    x_recv,
    z_stage_own,
    z_recv_own,
    z_stage,
    z_recv,
    wmt,
    wzt,
    wm,
    wz,
    wzo,
    lanes_m,
    lanes_z,
    lanes_zo,
    scale,
    base,
    total,
    local_sem,
    ask_send,
    ask_recv,
    list_send,
    list_recv,
    hop1_send,
    hop1_recv,
    hop2_send,
    hop2_recv,
    x_send,
    x_got,
    z_send,
    z_got,
):
    chunks = len(CHUNKS)
    starts = [sum(CHUNKS[:c]) for c in range(chunks)]
    dom = lax.axis_index("dom")
    blk = lax.axis_index("blk")
    low, z = dom // GROUP, dom % GROUP
    high, j = blk // GROUP, blk % GROUP
    other_dom = (dom + GROUP) % (2 * GROUP)
    other_blk = (blk + GROUP) % (2 * GROUP)
    partner = (other_dom, blk)
    beyond = (other_dom, other_blk)

    def row_peer(d):
        return (dom, high * GROUP + (j + d) % GROUP)

    def z_peer(d):
        return (low * GROUP + (z + d) % GROUP, blk)

    loads = [
        (cols_hbm, colmsg),
        (list_hbm, listmsg),
        (list_hbm, slist),
        (cols_hbm, icols),
        (labels, panel),
        (rows_hbm, irows),
        (slot_hbm, cslot),
        (crow_hbm, crows),
        (seeds, seedv),
        (cut, wc),
        (intra, wi),
        (tags, prior),
    ]
    loads = [
        pltpu.make_async_copy(src, dst, local_sem.at[i])
        for i, (src, dst) in enumerate(loads)
    ]
    for load in loads:
        load.start()

    barrier = pltpu.get_barrier_semaphore()

    def greet(d, carry):
        pl.semaphore_signal(barrier, inc=1, device_id=row_peer(d), device_id_type=MESH)
        pl.semaphore_signal(barrier, inc=1, device_id=z_peer(d), device_id_type=MESH)
        return carry

    pl.semaphore_signal(barrier, inc=1, device_id=partner, device_id_type=MESH)
    pl.semaphore_signal(barrier, inc=1, device_id=beyond, device_id_type=MESH)
    lax.fori_loop(1, GROUP, greet, 0)
    loads[0].wait()
    loads[1].wait()
    pl.semaphore_wait(barrier, 2 * GROUP)

    def ask(d):
        return pltpu.make_async_remote_copy(
            src_ref=colmsg,
            dst_ref=request_land.at[j],
            send_sem=ask_send.at[d],
            recv_sem=ask_recv.at[d],
            device_id=row_peer(d),
            device_id_type=MESH,
        )

    def ask_arrival(d):
        return pltpu.make_async_remote_copy(
            src_ref=colmsg,
            dst_ref=request_land.at[(j + GROUP - d) % GROUP],
            send_sem=ask_send.at[d],
            recv_sem=ask_recv.at[d],
            device_id=row_peer(d),
            device_id_type=MESH,
        )

    def start_ask(d, carry):
        ask(d).start()
        return carry

    lax.fori_loop(1, GROUP, start_ask, 0)
    tell = pltpu.make_async_remote_copy(
        src_ref=listmsg,
        dst_ref=list_land,
        send_sem=list_send,
        recv_sem=list_recv,
        device_id=partner,
        device_id_type=MESH,
    )
    tell.start()

    hop1 = [
        pltpu.make_async_remote_copy(
            src_ref=labels.at[:, pl.ds(starts[c], CHUNKS[c])],
            dst_ref=partner_parts[c],
            send_sem=hop1_send.at[c],
            recv_sem=hop1_recv.at[c],
            device_id=partner,
            device_id_type=MESH,
        )
        for c in range(chunks)
    ]
    hop2 = [
        pltpu.make_async_remote_copy(
            src_ref=partner_parts[c],
            dst_ref=mirror_parts[c],
            send_sem=hop2_send.at[c],
            recv_sem=hop2_recv.at[c],
            device_id=beyond,
            device_id_type=MESH,
        )
        for c in range(chunks)
    ]
    for c in range(min(WINDOW, chunks)):
        hop1[c].start()

    def spread_order(i):
        return 1 + (i + 3) % (GROUP - 1)

    def z_copy(stage, recv, index, d, slot):
        return pltpu.make_async_remote_copy(
            src_ref=stage.at[d],
            dst_ref=recv.at[slot],
            send_sem=z_send.at[index, d],
            recv_sem=z_got.at[index, d],
            device_id=z_peer(d),
            device_id_type=MESH,
        )

    def x_copy(stage, recv, index, d, slot):
        return pltpu.make_async_remote_copy(
            src_ref=stage.at[d],
            dst_ref=recv.at[slot],
            send_sem=x_send.at[index, d],
            recv_sem=x_got.at[index, d],
            device_id=row_peer(d),
            device_id_type=MESH,
        )

    def z_serve(source, wanted, stage, recv, index):
        def one(i, carry):
            d = spread_order(i)
            stage[d] = source[wanted[0, low * GROUP + (z + d) % GROUP]]
            z_copy(stage, recv, index, d, z).start()
            return carry

        lax.fori_loop(0, GROUP - 1, one, 0)
        recv[z] = source[wanted[0, dom]]

    def x_serve(source, which, stage, recv, index):
        def one(i, carry):
            d = spread_order(i)
            peer = (j + d) % GROUP
            stage[d, 0] = source[requests[peer, 0, which]]
            stage[d, 1] = source[requests[peer, 1, which]]
            x_copy(stage, recv, index, d, j).start()
            return carry

        lax.fori_loop(0, GROUP - 1, one, 0)
        recv[j, 0] = source[icols[0, which]]
        recv[j, 1] = source[icols[1, which]]

    def z_wait(stage, recv, index):
        def one(d, carry):
            z_copy(stage, recv, index, d, (z + GROUP - d) % GROUP).wait_recv()
            return carry

        lax.fori_loop(1, GROUP, one, 0)

    def x_wait(stage, recv, index):
        def one(d, carry):
            x_copy(stage, recv, index, d, (j + GROUP - d) % GROUP).wait_recv()
            return carry

        lax.fori_loop(1, GROUP, one, 0)

    for load in loads[2:5]:
        load.wait()
    z_serve(panel, slist, z_stage_own, z_recv_own, chunks)

    def take_ask(d, carry):
        ask_arrival(d).wait_recv()
        return carry

    lax.fori_loop(1, GROUP, take_ask, 0)
    request_land[j] = colmsg[...]
    settle = pltpu.make_async_copy(request_land, requests, local_sem.at[0])
    settle.start()
    settle.wait()
    x_serve(panel, blk, x_stage_own, x_recv_own, chunks)

    def lane_index(width):
        return lax.broadcasted_iota(I32, (GRAIN, width), 1)

    def prepare_cut():
        for load in loads[5:10]:
            load.wait()

        def invert(q, carry):
            found = jnp.int32(0)
            for k in range(TILES):
                found = jnp.where(cslot[0, k] == q, k, found)
            inverse[q] = found
            return carry

        lax.fori_loop(0, TILES, invert, 0)
        lane = lane_index(WIDTH)
        for b in range(GROUP // 2):
            k0 = inverse[low * GROUP + 2 * b]
            k1 = inverse[low * GROUP + 2 * b + 1]
            wzo[b, :, 0:EDGE] = wc[k0]
            wzo[b, :, EDGE : 2 * EDGE] = wc[k1]
            lanes_zo[b] = jnp.where(lane < EDGE, crows[0, k0], crows[0, k1])
        lane = lane_index(GROUP * GRAIN) // GRAIN
        ids = jnp.zeros((GRAIN, GROUP * GRAIN), I32)
        for q in range(GROUP):
            ids = jnp.where(lane == q, crows[0, inverse[(1 - low) * GROUP + q]], ids)
        lanes_z[...] = ids

        def turn(q, carry):
            flipped = wc[inverse[(1 - low) * GROUP + q]].T
            for c in range(TILES // 2):
                wzt[c, pl.ds(pl.multiple_of(q * GRAIN, GRAIN), GRAIN), :] = flipped[
                    c * GRAIN : (c + 1) * GRAIN, :
                ]
            return carry

        lax.fori_loop(0, GROUP, turn, 0)

        def back(c, carry):
            wz[c] = wzt[c].T
            return carry

        lax.fori_loop(0, TILES // 2, back, 0)

    def prepare_mirror():
        loads[10].wait()
        lane = lane_index(2 * GROUP * GRAIN) // GRAIN
        ids = jnp.zeros((GRAIN, 2 * GROUP * GRAIN), I32)
        for p in range(GROUP):
            for k in range(2):
                ids = jnp.where(
                    lane == 2 * p + k, irows[k, (1 - high) * GROUP + p], ids
                )
        lanes_m[...] = ids

        def turn(p, carry):
            for k in range(2):
                flipped = wi[(1 - high) * GROUP + p, k].T
                for c in range(TILES // 2):
                    wmt[
                        c,
                        pl.ds(pl.multiple_of((2 * p + k) * GRAIN, GRAIN), GRAIN),
                        :,
                    ] = flipped[c * GRAIN : (c + 1) * GRAIN, :]
            return carry

        lax.fori_loop(0, GROUP, turn, 0)

        def back(c, carry):
            wm[c, :, 0:EDGE] = wmt[c, 0:EDGE, :].T
            wm[c, :, EDGE : 2 * EDGE] = wmt[c, EDGE : 2 * EDGE, :].T
            return carry

        lax.fori_loop(0, TILES // 2, back, 0)

    def prepare_scale():
        tile = lax.broadcasted_iota(I32, (EDGE, 2 * EDGE), 0)
        lane = lax.broadcasted_iota(I32, (EDGE, 2 * EDGE), 1)

        def sums(weights, row0, row1):
            chosen = jnp.where(tile == jnp.where(lane < EDGE, row0, row1), 1.0, 0.0)
            return lax.dot_general(
                weights,
                chosen.astype(BF16),
                (((1,), (1,)), ((), ())),
                preferred_element_type=F32,
            )

        def intra_sums(s, degree):
            weights = jnp.concatenate([wi[s, 0], wi[s, 1]], axis=1)
            return degree + sums(weights, irows[0, s], irows[1, s])

        def cut_sums(h, degree):
            weights = jnp.concatenate([wc[2 * h], wc[2 * h + 1]], axis=1)
            return degree + sums(weights, crows[0, 2 * h], crows[0, 2 * h + 1])

        degree = lax.fori_loop(0, TILES, intra_sums, jnp.zeros((EDGE, EDGE), F32))
        degree = lax.fori_loop(0, TILES // 2, cut_sums, degree)
        used = lax.broadcasted_iota(I32, (EDGE, EDGE), 1) < TILES
        mask = jnp.concatenate(
            [seedv[...].astype(F32), jnp.zeros((EDGE - TILES, EDGE), F32)], axis=0
        ).T
        factor = jnp.where(mask > 0.5, 0.0, ALPHA / jnp.where(used, degree, 1.0))
        rest = jnp.where(mask > 0.5, 1.0, 1.0 - ALPHA)
        loads[11].wait()
        for t in range(TILES):
            scale[t] = jnp.broadcast_to(factor[:, t : t + 1], (EDGE, EDGE))
            share = jnp.broadcast_to(rest[:, t : t + 1], (EDGE, EDGE))
            share = jnp.concatenate([share, share], axis=1)
            base[t] = prior[t].astype(F32) * share

    span = 4

    def spread_part(tg, blocks):
        part = None
        for weights, ids, values in blocks:
            pieces = []
            width = weights.shape[1]
            cube = weights.reshape(EDGE // GRAIN, GRAIN, width)
            for u in range(span):
                keep = jnp.where(ids == tg * span + u, 1.0, 0.0).astype(BF16)
                pieces.append((cube * keep[None]).reshape(EDGE, width))
            lhs = jnp.concatenate(pieces, axis=0)
            term = jnp.dot(lhs, values, preferred_element_type=F32)
            part = term if part is None else part + term
        return part

    def gather_own_x(first, count):
        def one(tg, carry):
            lane = lane_index(WIDTH)
            blocks = []
            for p in range(first, first + count):
                s = high * GROUP + p
                ids = jnp.where(lane < EDGE, irows[0, s], irows[1, s])
                weights = jnp.concatenate([wi[s, 0], wi[s, 1]], axis=1)
                values = x_recv_own[p].reshape(2 * EDGE, WIDTH)
                blocks.append((weights, ids, values))
            at = pl.ds(pl.multiple_of(tg * span * EDGE, EDGE), span * EDGE)
            total[at, :] += spread_part(tg, blocks)
            return carry

        lax.fori_loop(0, TILES // span, one, 0)

    def gather_own_z():
        z_wait(z_stage_own, z_recv_own, chunks)

        def one(tg, carry):
            blocks = []
            for b in range(GROUP // 2):
                values = z_recv_own[2 * b : 2 * b + 2].reshape(2 * EDGE, WIDTH)
                blocks.append((wzo[b], lanes_zo[b], values))
            at = pl.ds(pl.multiple_of(tg * span * EDGE, EDGE), span * EDGE)
            total[at, :] = spread_part(tg, blocks)
            return carry

        lax.fori_loop(0, TILES // span, one, 0)

    def chunk_blocks(c):
        return [
            (wm[c], lanes_m[...], x_recv[c][...].reshape(2 * GROUP * GRAIN, WIDTH)),
            (wz[c], lanes_z[...], z_recv[c][...].reshape(GROUP * GRAIN, WIDTH)),
        ]

    def gather_chunks(cs):
        for c in cs:
            z_wait(z_stage[c], z_recv[c], c)
            x_wait(x_stage[c], x_recv[c], c)

        def one(tg, carry):
            blocks = []
            for c in cs:
                blocks += chunk_blocks(c)
            at = pl.ds(pl.multiple_of(tg * span * EDGE, EDGE), span * EDGE)
            total[at, :] += spread_part(tg, blocks)
            return carry

        lax.fori_loop(0, TILES // span, one, 0)

    def finish(c):
        z_wait(z_stage[c], z_recv[c], c)
        x_wait(x_stage[c], x_recv[c], c)

        def one(tg, carry):
            at = pl.ds(pl.multiple_of(tg * span * EDGE, EDGE), span * EDGE)
            spread = total[at, :] + spread_part(tg, chunk_blocks(c))
            factor = scale[pl.ds(tg * span, span)].reshape(span * EDGE, EDGE)
            factor = jnp.concatenate([factor, factor], axis=1)
            rest = base[pl.ds(tg * span, span)].reshape(span * EDGE, WIDTH)
            out[at, :] = (factor * spread + rest).astype(BF16)
            return carry

        lax.fori_loop(0, TILES // span, one, 0)

    def own_x_first():
        x_wait(x_stage_own, x_recv_own, chunks)
        gather_own_x(0, 4)

    work = {
        0: [prepare_cut],
        1: [prepare_mirror],
        2: [prepare_scale],
        3: [],
        4: [gather_own_z],
        5: [own_x_first],
        6: [lambda: gather_own_x(4, 4)],
        7: [lambda: gather_chunks([0, 1, 2, 3])],
        8: [lambda: gather_chunks([4, 5]), lambda: gather_chunks([6])],
    }
    for c in range(chunks + 1):
        if c < chunks:
            hop1[c].wait_recv()
            hop2[c].start()
            if c + WINDOW < chunks:
                hop1[c].wait_send()
                hop1[c + WINDOW].start()
            if c == 0:
                tell.wait_recv()
                settle = pltpu.make_async_copy(list_land, partner_list, local_sem.at[0])
                settle.start()
                settle.wait()
            z_serve(partner_parts[c], partner_list, z_stage[c], z_recv[c], c)
        if c >= 1:
            hop2[c - 1].wait_recv()
            x_serve(mirror_parts[c - 1], other_blk, x_stage[c - 1], x_recv[c - 1], c - 1)
        for piece in work[c]:
            piece()
    finish(chunks - 1)

    def left(d, carry):
        ask(d).wait_send()
        z_copy(z_stage_own, z_recv_own, chunks, d, z).wait_send()
        x_copy(x_stage_own, x_recv_own, chunks, d, j).wait_send()
        for c in range(chunks):
            z_copy(z_stage[c], z_recv[c], c, d, z).wait_send()
            x_copy(x_stage[c], x_recv[c], c, d, j).wait_send()
        return carry

    lax.fori_loop(1, GROUP, left, 0)
    tell.wait_send()
    for c in range(chunks):
        if c + WINDOW >= chunks:
            hop1[c].wait_send()
        hop2[c].wait_send()


def on_device(
    labels,
    tags,
    seed_mask,
    intra_tiles,
    intra_rows,
    intra_cols,
    send_list,
    cut_tiles,
    cut_slot,
    cut_rows,
):
    chunks = len(CHUNKS)

    def flat(ids):
        return jnp.swapaxes(ids[0], 0, 1)

    parts = EDGE // GRAIN
    operands = (
        labels.reshape(TILES, parts, GRAIN, WIDTH),
        tags.reshape(TILES, EDGE, WIDTH),
        seed_mask.reshape(TILES, EDGE),
        intra_tiles.reshape(TILES, 2, EDGE, EDGE),
        cut_tiles.reshape(TILES, EDGE, EDGE),
        flat(intra_rows),
        flat(intra_cols),
        flat(send_list),
        cut_slot,
        cut_rows,
    )
    vmem = pltpu.VMEM
    smem = pltpu.SMEM

    def per_chunk(*shape):
        return [
            vmem(tuple(g if n is None else n for n in shape), BF16) for g in CHUNKS
        ]

    scratch = [
        vmem((TILES, parts, GRAIN, WIDTH), BF16),
        vmem((TILES, EDGE, WIDTH), BF16),
        vmem((TILES, EDGE), I32),
        vmem((TILES, 2, EDGE, EDGE), BF16),
        vmem((TILES, EDGE, EDGE), BF16),
        smem((2, TILES), I32),
        smem((2, TILES), I32),
        smem((1, TILES), I32),
        smem((1, TILES), I32),
        smem((1, TILES), I32),
        vmem((2, TILES), I32),
        vmem((1, TILES), I32),
        vmem((GROUP, 2, TILES), I32),
        vmem((1, TILES), I32),
        smem((GROUP, 2, TILES), I32),
        smem((1, TILES), I32),
        smem((TILES,), I32),
        per_chunk(TILES, None, GRAIN, WIDTH),
        per_chunk(TILES, None, GRAIN, WIDTH),
        vmem((GROUP, 2, parts, GRAIN, WIDTH), BF16),
        vmem((GROUP, 2, parts, GRAIN, WIDTH), BF16),
        per_chunk(GROUP, 2, None, GRAIN, WIDTH),
        per_chunk(GROUP, 2, None, GRAIN, WIDTH),
        vmem((GROUP, parts, GRAIN, WIDTH), BF16),
        vmem((GROUP, parts, GRAIN, WIDTH), BF16),
        per_chunk(GROUP, None, GRAIN, WIDTH),
        per_chunk(GROUP, None, GRAIN, WIDTH),
        vmem((parts, 2 * GROUP * GRAIN, EDGE), BF16),
        vmem((parts, GROUP * GRAIN, EDGE), BF16),
        vmem((parts, EDGE, 2 * GROUP * GRAIN), BF16),
        vmem((parts, EDGE, GROUP * GRAIN), BF16),
        vmem((GROUP // 2, EDGE, 2 * EDGE), BF16),
        vmem((GRAIN, 2 * GROUP * GRAIN), I32),
        vmem((GRAIN, GROUP * GRAIN), I32),
        vmem((GROUP // 2, GRAIN, 2 * EDGE), I32),
        vmem((TILES, EDGE, EDGE), F32),
        vmem((TILES, EDGE, WIDTH), F32),
        vmem((TILES * EDGE, WIDTH), F32),
        pltpu.SemaphoreType.DMA((12,)),
        pltpu.SemaphoreType.DMA((GROUP,)),
        pltpu.SemaphoreType.DMA((GROUP,)),
        pltpu.SemaphoreType.DMA,
        pltpu.SemaphoreType.DMA,
        pltpu.SemaphoreType.DMA((chunks,)),
        pltpu.SemaphoreType.DMA((chunks,)),
        pltpu.SemaphoreType.DMA((chunks,)),
        pltpu.SemaphoreType.DMA((chunks,)),
        pltpu.SemaphoreType.DMA((chunks + 1, GROUP)),
        pltpu.SemaphoreType.DMA((chunks + 1, GROUP)),
        pltpu.SemaphoreType.DMA((chunks + 1, GROUP)),
        pltpu.SemaphoreType.DMA((chunks + 1, GROUP)),
    ]
    return pl.pallas_call(
        kernel,
        out_shape=jax.ShapeDtypeStruct((TILES * EDGE, WIDTH), BF16),
        in_specs=[pl.BlockSpec(memory_space=pl.ANY)] * len(operands),
        out_specs=pl.BlockSpec(memory_space=pltpu.VMEM),
        scratch_shapes=scratch,
        compiler_params=pltpu.CompilerParams(
            collective_id=0, has_side_effects=True, vmem_limit_bytes=62 * 2**20
        ),
        name="propagate",
    )(*operands)


def solution(mesh):
    both = ("dom", "blk")
    placed = (
        P(both, None),
        P(both, None),
        P(both),
        P(both, None, None, None, None),
        P(both, None, None),
        P(both, None, None),
        P(both, None, None),
        P(both, None, None, None),
        P(both, None),
        P(both, None),
    )
    return jax.shard_map(
        on_device, mesh=mesh, in_specs=placed, out_specs=P(both, None), check_vma=False
    )
```

time: 315 us -> 59.5 us (0.19)
  the two profiles are of different devices: /device:TPU:32 before, /device:TPU:1 now
where the time goes in v1:
time: 59.5 us; the launch traced here: 59.4 us
  Pallas kernels  57.2 us (96%)
  local copies, waits for them, and re-layouts  2.26 us (4%)
    pallas_call x1, Pallas kernels, on_device(): pl.pallas_call(kernel, out_shape=jax.ShapeDtypeStruct((TILES * EDGE, WIDT...  57.2 us
    unnamed x1, local copies, waits for them, and re-layouts  2.26 us

profile of v1, /device:TPU:1, one launch (start us, length us, event | category | flops | bytes accessed | tf_op | source)
XLA Modules:
  0.0 59.4 jit_solution(13999846105297701265)
XLA Ops:
  0.0 57.2 %propagate.1 = bf16[2048,256]{1,0:T(8,128)(2,1)} custom-call(bf16[16,8,16,256]{3,2,1,0:T(8,128)(2,1)} %bitcast.12, bf16[16,128,256]{2,1,0:T(8,128)(2,1)} %bitcast.13, s32[16,128]{1,0:T(8,128)} %bitcast.16, bf16[16,2,128,128]{3,2,1,0:T(8,128)(2,1)} %bitcast.14, bf16[16,128,128]{2,1,0:T(8,128)(2,1)} %bitcast.15, s32[2,16]{1,0:T(2,128)} %bitcast.17, ...), custom_call_target="tpu_custom_call" | custom-call | tf_op jit(solution)/shard_map/propagate/pallas_call | solution.py:611
  57.2 2.3 %copy.12 = bf16[2048,256]{1,0:T(8,128)(2,1)} copy(bf16[2048,256]{1,0:T(8,128)(2,1)} %propagate.1) | data formatting | bytes 2097152

commit v2 on v1

v2 whole, which is shorter than its diff:
```python
import jax
import jax.numpy as jnp
from jax import lax
from jax.experimental import pallas as pl
from jax.experimental.pallas import tpu as pltpu
from jax.sharding import PartitionSpec as P

ALPHA = 0.8
MESH = pl.DeviceIdType.MESH
F32 = jnp.float32
BF16 = jnp.bfloat16
I32 = jnp.int32
TILES = 16
EDGE = 128
WIDTH = 256
GRAIN = 16
PARTS = EDGE // GRAIN
GROUP = 8
SPAN = 4
CHUNKS = (1, 1, 1, 1, 1, 1, 1, 1)


def kernel(
    labels,
    tags,
    seeds,
    intra,
    cut,
    rows_hbm,
    cols_hbm,
    list_hbm,
    slot_hbm,
    crow_hbm,
    out,
    panel,
    prior,
    seedv,
    wi,
    wc,
    irows,
    icols,
    slist,
    cslot,
    crows,
    colmsg,
    listmsg,
    request_land,
    list_land,
    requests,
    partner_list,
    partner_parts,
    mirror_parts,
    x_stage_own,
    x_recv_own,
    x_stage,
    x_recv,
    z_stage_own,
    z_stage,
    z_recv,
    wmt,
    wm,
    lanes_m,
    degree,
    scale,
    base,
    total,
    local_sem,
    ask_send,
    ask_recv,
    list_send,
    list_recv,
    hop1_send,
    hop1_recv,
    hop2_send,
    hop2_recv,
    x_send,
    x_got,
    z_send,
    z_got,
):
    chunks = len(CHUNKS)
    own = chunks
    starts = [sum(CHUNKS[:c]) for c in range(chunks)]
    dom = lax.axis_index("dom")
    blk = lax.axis_index("blk")
    low, z = dom // GROUP, dom % GROUP
    high, j = blk // GROUP, blk % GROUP
    other_dom = (dom + GROUP) % (2 * GROUP)
    other_blk = (blk + GROUP) % (2 * GROUP)
    partner = (other_dom, blk)
    beyond = (other_dom, other_blk)

    def row_peer(d):
        return (dom, high * GROUP + (j + d) % GROUP)

    def z_peer(d):
        return (low * GROUP + (z + d) % GROUP, blk)

    def remote(src, dst, send, recv, device):
        return pltpu.make_async_remote_copy(
            src_ref=src,
            dst_ref=dst,
            send_sem=send,
            recv_sem=recv,
            device_id=device,
            device_id_type=MESH,
        )

    loads = [
        (cols_hbm, colmsg),
        (list_hbm, listmsg),
        (list_hbm, slist),
        (labels, panel),
        (cols_hbm, icols),
        (rows_hbm, irows),
        (intra, wi),
        (slot_hbm, cslot),
        (crow_hbm, crows),
        (seeds, seedv),
        (cut, wc),
        (tags, prior),
    ]
    loads = [
        pltpu.make_async_copy(src, dst, local_sem.at[i])
        for i, (src, dst) in enumerate(loads)
    ]

    barrier = pltpu.get_barrier_semaphore()

    def greet(d, carry):
        pl.semaphore_signal(barrier, inc=1, device_id=row_peer(d), device_id_type=MESH)
        pl.semaphore_signal(barrier, inc=1, device_id=z_peer(d), device_id_type=MESH)
        return carry

    pl.semaphore_signal(barrier, inc=1, device_id=partner, device_id_type=MESH)
    pl.semaphore_signal(barrier, inc=1, device_id=beyond, device_id_type=MESH)
    lax.fori_loop(1, GROUP, greet, 0)
    for load in loads:
        load.start()
    for load in loads[0:3]:
        load.wait()
    pl.semaphore_wait(barrier, 2 * GROUP)

    def ask(d):
        return remote(
            colmsg, request_land.at[d], ask_send.at[d], ask_recv.at[d], row_peer(d)
        )

    def start_ask(d, carry):
        ask(d).start()
        return carry

    lax.fori_loop(1, GROUP, start_ask, 0)
    tell = remote(listmsg, list_land, list_send, list_recv, partner)
    tell.start()

    hop1 = [
        remote(
            labels.at[:, pl.ds(starts[c], CHUNKS[c])],
            partner_parts[c],
            hop1_send.at[c],
            hop1_recv.at[c],
            partner,
        )
        for c in range(chunks)
    ]
    hop2 = [
        remote(
            partner_parts[c],
            mirror_parts[c],
            hop2_send.at[c],
            hop2_recv.at[c],
            beyond,
        )
        for c in range(chunks)
    ]
    for c in range(chunks):
        hop1[c].start()

    others = pl.ds(1, GROUP - 1)

    def spread_order(i):
        return 1 + (i + 3) % (GROUP - 1)

    def z_refs(index, at):
        if index == own:
            return z_stage_own.at[at], z_recv.at[0, at]
        rows = pl.ds(starts[index], CHUNKS[index])
        return z_stage[index].at[at], z_recv.at[1, at, rows]

    def x_refs(index, at):
        if index == own:
            return x_stage_own.at[at], x_recv_own.at[at]
        return x_stage[index].at[at], x_recv[index].at[at]

    def z_copy(index, at, d):
        src, dst = z_refs(index, at)
        return remote(src, dst, z_send.at[index], z_got.at[index], z_peer(d))

    def x_copy(index, at, d):
        src, dst = x_refs(index, at)
        return remote(src, dst, x_send.at[index], x_got.at[index], row_peer(d))

    def z_serve(source, wanted, index):
        stage = z_stage_own if index == own else z_stage[index]

        def one(i, carry):
            d = spread_order(i)
            stage[d] = source[wanted[0, low * GROUP + (z + d) % GROUP]]
            z_copy(index, d, d).start()
            return carry

        lax.fori_loop(0, GROUP - 1, one, 0)
        mine = source[wanted[0, dom]]
        if index == own:
            z_recv[0, 0] = mine
        else:
            z_recv[1, 0, starts[index] : starts[index] + CHUNKS[index]] = mine

    def x_serve(source, which, index):
        stage, recv = (
            (x_stage_own, x_recv_own)
            if index == own
            else (x_stage[index], x_recv[index])
        )

        def one(i, carry):
            d = spread_order(i)
            stage[d, 0] = source[requests[GROUP - d, 0, which]]
            stage[d, 1] = source[requests[GROUP - d, 1, which]]
            x_copy(index, d, d).start()
            return carry

        lax.fori_loop(0, GROUP - 1, one, 0)
        recv[0, 0] = source[icols[0, which]]
        recv[0, 1] = source[icols[1, which]]

    def z_wait(index):
        z_copy(index, others, 1).wait_recv()

    def x_wait(index):
        x_copy(index, others, 1).wait_recv()

    loads[3].wait()
    z_serve(panel, slist, own)

    def take_ask(d, carry):
        ask(d).wait_recv()
        return carry

    lax.fori_loop(1, GROUP, take_ask, 0)
    settle = pltpu.make_async_copy(request_land, requests, local_sem.at[0])
    settle.start()
    loads[4].wait()
    settle.wait()
    x_serve(panel, blk, own)

    lane = lax.broadcasted_iota(I32, (GRAIN, 2 * EDGE), 1)

    def sender(d):
        return (j + GROUP - d) % GROUP

    def mirror_ids():
        loads[5].wait()
        loads[6].wait()
        slot = lane // GRAIN
        ids = jnp.zeros((GRAIN, 2 * EDGE), I32)
        for d in range(GROUP):
            for k in range(2):
                row = irows[k, (1 - high) * GROUP + sender(d)]
                ids = jnp.where(slot == 2 * d + k, row, ids)
        lanes_m[...] = ids

    def mirror_turn(first, count):
        def turn(d, carry):
            for k in range(2):
                flipped = wi[(1 - high) * GROUP + sender(d), k].T
                at = pl.ds(pl.multiple_of((2 * d + k) * GRAIN, GRAIN), GRAIN)
                for c in range(PARTS):
                    wmt[c, at, :] = flipped[c * GRAIN : (c + 1) * GRAIN, :]
            return carry

        lax.fori_loop(first, first + count, turn, 0)

    def mirror_back(first, count):
        def back(c, carry):
            wm[c, :, 0:EDGE] = wmt[c, 0:EDGE, :].T
            wm[c, :, EDGE : 2 * EDGE] = wmt[c, EDGE : 2 * EDGE, :].T
            return carry

        lax.fori_loop(first, first + count, back, 0)

    def sums(weights, row0, row1):
        tile = lax.broadcasted_iota(I32, (EDGE, 2 * EDGE), 0)
        wide = lax.broadcasted_iota(I32, (EDGE, 2 * EDGE), 1)
        chosen = jnp.where(tile == jnp.where(wide < EDGE, row0, row1), 1.0, 0.0)
        return lax.dot_general(
            weights,
            chosen.astype(BF16),
            (((1,), (1,)), ((), ())),
            preferred_element_type=F32,
        )

    def intra_degree(first, count):
        def one(s, value):
            weights = jnp.concatenate([wi[s, 0], wi[s, 1]], axis=1)
            return value + sums(weights, irows[0, s], irows[1, s])

        start = degree[...] if first else jnp.zeros((EDGE, EDGE), F32)
        degree[...] = lax.fori_loop(first, first + count, one, start)

    def cut_degree():
        for load in loads[7:12]:
            load.wait()

        def one(h, value):
            weights = jnp.concatenate([wc[2 * h], wc[2 * h + 1]], axis=1)
            return value + sums(weights, crows[0, 2 * h], crows[0, 2 * h + 1])

        degree[...] = lax.fori_loop(0, TILES // 2, one, degree[...])

    def set_scale(first, count):
        used = lax.broadcasted_iota(I32, (EDGE, EDGE), 1) < TILES
        mask = jnp.concatenate(
            [seedv[...].astype(F32), jnp.zeros((EDGE - TILES, EDGE), F32)], axis=0
        ).T
        factor = jnp.where(mask > 0.5, 0.0, ALPHA / jnp.where(used, degree[...], 1.0))
        rest = jnp.where(mask > 0.5, 1.0, 1.0 - ALPHA)
        for t in range(first, first + count):
            scale[t] = jnp.broadcast_to(factor[:, t : t + 1], (EDGE, EDGE))
            share = jnp.broadcast_to(rest[:, t : t + 1], (EDGE, EDGE))
            share = jnp.concatenate([share, share], axis=1)
            base[t] = prior[t].astype(F32) * share

    def spread_part(tg, blocks):
        part = None
        for weights, ids, values in blocks:
            pieces = []
            width = weights.shape[1]
            cube = weights.reshape(PARTS, GRAIN, width)
            for u in range(SPAN):
                keep = jnp.where(ids == tg * SPAN + u, 1.0, 0.0).astype(BF16)
                pieces.append((cube * keep[None]).reshape(EDGE, width))
            lhs = jnp.concatenate(pieces, axis=0)
            term = jnp.dot(lhs, values, preferred_element_type=F32)
            part = term if part is None else part + term
        return part

    def row_span(tg):
        return pl.ds(pl.multiple_of(tg * SPAN * EDGE, EDGE), SPAN * EDGE)

    def own_x(first, count, lo, hi):
        def one(tg, carry):
            blocks = []
            for d in range(first, first + count):
                s = high * GROUP + sender(d)
                ids = jnp.where(lane < EDGE, irows[0, s], irows[1, s])
                weights = jnp.concatenate([wi[s, 0], wi[s, 1]], axis=1)
                values = x_recv_own[d].reshape(2 * EDGE, WIDTH)
                blocks.append((weights, ids, values))
            part = spread_part(tg, blocks)
            if first == 0:
                total[row_span(tg), :] = part
            else:
                total[row_span(tg), :] += part
            return carry

        lax.fori_loop(lo, hi, one, 0)

    def chunk_blocks(c):
        return [
            (
                wm[starts[c] + g],
                lanes_m[...],
                x_recv[c][:, :, g].reshape(2 * EDGE, WIDTH),
            )
            for g in range(CHUNKS[c])
        ]

    def mirror_x(cs):
        def one(tg, carry):
            blocks = []
            for c in cs:
                blocks += chunk_blocks(c)
            total[row_span(tg), :] += spread_part(tg, blocks)
            return carry

        lax.fori_loop(0, TILES // SPAN, one, 0)

    def add_cut():
        def one(t, carry):
            k = (t + TILES - crows[0, 0]) % TILES
            q = cslot[0, k]
            group = jnp.where(q // GROUP == low, 0, 1)
            block = z_recv[group, (z + GROUP - q % GROUP) % GROUP]
            at = pl.ds(pl.multiple_of(t * EDGE, EDGE), EDGE)
            total[at, :] += jnp.dot(
                wc[k], block.reshape(EDGE, WIDTH), preferred_element_type=F32
            )
            return carry

        lax.fori_loop(0, TILES, one, 0, unroll=2)

    def finish(c):
        def one(tg, carry):
            at = row_span(tg)
            spread = total[at, :] + spread_part(tg, chunk_blocks(c))
            factor = scale[pl.ds(tg * SPAN, SPAN)].reshape(SPAN * EDGE, EDGE)
            factor = jnp.concatenate([factor, factor], axis=1)
            rest = base[pl.ds(tg * SPAN, SPAN)].reshape(SPAN * EDGE, WIDTH)
            out[at, :] = (factor * spread + rest).astype(BF16)
            return carry

        lax.fori_loop(0, TILES // SPAN, one, 0)

    def many(*pieces):
        def run():
            for piece in pieces:
                piece()

        return run

    work = [
        [(mirror_ids,), (mirror_turn, 0, 4)],
        [(mirror_turn, 4, 4), (mirror_back, 0, 4)],
        [(mirror_back, 4, 4), (intra_degree, 0, 16)],
        [(cut_degree,), (set_scale, 0, 4)],
        [(set_scale, 4, 12)],
        [(x_wait, own), (own_x, 0, 4, 0, 4)],
        [(own_x, 4, 4, 0, 4)],
        [(x_wait, 0), (x_wait, 1), (x_wait, 2), (x_wait, 3), (mirror_x, [0, 1, 2, 3])],
        [(x_wait, 4), (x_wait, 5), (mirror_x, [4, 5]), (x_wait, 6), (mirror_x, [6])],
    ]
    for c in range(chunks + 1):
        if c < chunks:
            hop1[c].wait_recv()
            hop2[c].start()
            if c == 0:
                tell.wait_recv()
                settle = pltpu.make_async_copy(list_land, partner_list, local_sem.at[1])
                settle.start()
                settle.wait()
            z_serve(partner_parts[c], partner_list, c)
        if c >= 1:
            hop2[c - 1].wait_recv()
            x_serve(mirror_parts[c - 1], other_blk, c - 1)
        for piece, *given in work[c]:
            piece(*given)
    z_wait(own)
    for c in range(chunks):
        z_wait(c)
    add_cut()
    x_wait(chunks - 1)
    finish(chunks - 1)

    def left(d, carry):
        ask(d).wait_send()
        return carry

    lax.fori_loop(1, GROUP, left, 0)
    tell.wait_send()
    for c in range(chunks + 1):
        z_copy(c, others, 1).wait_send()
        x_copy(c, others, 1).wait_send()
    for c in range(chunks):
        hop1[c].wait_send()
        hop2[c].wait_send()


def on_device(
    labels,
    tags,
    seed_mask,
    intra_tiles,
    intra_rows,
    intra_cols,
    send_list,
    cut_tiles,
    cut_slot,
    cut_rows,
):
    chunks = len(CHUNKS)

    def flat(ids):
        return jnp.swapaxes(ids[0], 0, 1)

    operands = (
        labels.reshape(TILES, PARTS, GRAIN, WIDTH),
        tags.reshape(TILES, EDGE, WIDTH),
        seed_mask.reshape(TILES, EDGE),
        intra_tiles.reshape(TILES, 2, EDGE, EDGE),
        cut_tiles.reshape(TILES, EDGE, EDGE),
        flat(intra_rows),
        flat(intra_cols),
        flat(send_list),
        cut_slot,
        cut_rows,
    )
    operands = [pltpu.with_memory_space_constraint(x, pltpu.HBM) for x in operands]
    vmem = pltpu.VMEM
    smem = pltpu.SMEM
    dma = pltpu.SemaphoreType.DMA

    def per_chunk(*shape):
        return [
            vmem(tuple(g if n is None else n for n in shape), BF16) for g in CHUNKS
        ]

    scratch = [
        vmem((TILES, PARTS, GRAIN, WIDTH), BF16),
        vmem((TILES, EDGE, WIDTH), BF16),
        vmem((TILES, EDGE), I32),
        vmem((TILES, 2, EDGE, EDGE), BF16),
        vmem((TILES, EDGE, EDGE), BF16),
        smem((2, TILES), I32),
        smem((2, TILES), I32),
        smem((1, TILES), I32),
        smem((1, TILES), I32),
        smem((1, TILES), I32),
        vmem((2, TILES), I32),
        vmem((1, TILES), I32),
        vmem((GROUP, 2, TILES), I32),
        vmem((1, TILES), I32),
        smem((GROUP, 2, TILES), I32),
        smem((1, TILES), I32),
        per_chunk(TILES, None, GRAIN, WIDTH),
        per_chunk(TILES, None, GRAIN, WIDTH),
        vmem((GROUP, 2, PARTS, GRAIN, WIDTH), BF16),
        vmem((GROUP, 2, PARTS, GRAIN, WIDTH), BF16),
        per_chunk(GROUP, 2, None, GRAIN, WIDTH),
        per_chunk(GROUP, 2, None, GRAIN, WIDTH),
        vmem((GROUP, PARTS, GRAIN, WIDTH), BF16),
        per_chunk(GROUP, None, GRAIN, WIDTH),
        vmem((2, GROUP, PARTS, GRAIN, WIDTH), BF16),
        vmem((PARTS, 2 * EDGE, EDGE), BF16),
        vmem((PARTS, EDGE, 2 * EDGE), BF16),
        vmem((GRAIN, 2 * EDGE), I32),
        vmem((EDGE, EDGE), F32),
        vmem((TILES, EDGE, EDGE), F32),
        vmem((TILES, EDGE, WIDTH), F32),
        vmem((TILES * EDGE, WIDTH), F32),
        dma((12,)),
        dma((GROUP,)),
        dma((GROUP,)),
        dma,
        dma,
        dma((chunks,)),
        dma((chunks,)),
        dma((chunks,)),
        dma((chunks,)),
        dma((chunks + 1,)),
        dma((chunks + 1,)),
        dma((chunks + 1,)),
        dma((chunks + 1,)),
    ]
    return pl.pallas_call(
        kernel,
        out_shape=pltpu.VMEM((TILES * EDGE, WIDTH), BF16),
        in_specs=[pl.BlockSpec(memory_space=pl.ANY)] * len(operands),
        out_specs=pl.BlockSpec(memory_space=pltpu.VMEM),
        scratch_shapes=scratch,
        compiler_params=pltpu.CompilerParams(
            collective_id=0, has_side_effects=True, vmem_limit_bytes=40 * 2**20
        ),
        name="propagate",
    )(*operands)


def solution(mesh):
    both = ("dom", "blk")
    placed = (
        P(both, None),
        P(both, None),
        P(both),
        P(both, None, None, None, None),
        P(both, None, None),
        P(both, None, None),
        P(both, None, None),
        P(both, None, None, None),
        P(both, None),
        P(both, None),
    )
    return jax.shard_map(
        on_device, mesh=mesh, in_specs=placed, out_specs=P(both, None), check_vma=False
    )
```

time: 59.5 us -> 51.3 us (0.86)
  Pallas kernels: 57.2 us -> 50.2 us
  local copies, waits for them, and re-layouts: 2.26 us -> 0.97 us
    pallas_call x1, Pallas kernels: 57.2 us -> 50.2 us  [on_device(): pl.pallas_call(kernel, out_shape=pltpu.VMEM((TILES * EDGE, WIDTH), BF16),...]
    unnamed x1, local copies, waits for them, and re-layouts: 2.26 us -> 0.97 us
where the time goes in v2:
time: 51.3 us; the launch traced here: 51.2 us
  Pallas kernels  50.2 us (98%)
  local copies, waits for them, and re-layouts  0.97 us (2%)
    pallas_call x1, Pallas kernels, on_device(): pl.pallas_call(kernel, out_shape=pltpu.VMEM((TILES * EDGE, WIDTH), BF16),...  50.2 us

profile of v2, /device:TPU:1, one launch (start us, length us, event | category | flops | bytes accessed | tf_op | source)
XLA Modules:
  0.0 51.2 jit_solution(9738888354760986305)
XLA Ops:
  0.0 50.2 %propagate.1 = bf16[2048,256]{1,0:T(8,128)(2,1)S(1)} custom-call(bf16[16,8,16,256]{3,2,1,0:T(8,128)(2,1)} %bitcast.12, bf16[16,128,256]{2,1,0:T(8,128)(2,1)} %bitcast.13, s32[16,128]{1,0:T(8,128)} %bitcast.16, bf16[16,2,128,128]{3,2,1,0:T(8,128)(2,1)} %bitcast.14, bf16[16,128,128]{2,1,0:T(8,128)(2,1)} %bitcast.15, s32[2,16]{1,0:T(2,128)} %bitcast.17, ...), custom_call_target="tpu_custom_call" | custom-call | tf_op jit(solution)/shard_map/propagate/pallas_call | solution.py:556
  50.2 1.0 %copy.12 = bf16[2048,256]{1,0:T(8,128)(2,1)} copy(bf16[2048,256]{1,0:T(8,128)(2,1)S(1)} %propagate.1) | data formatting | bytes 2097152

commit v3 on v2

--- a/solution.py
+++ b/solution.py
@@ -17,7 +17,9 @@
 PARTS = EDGE // GRAIN
 GROUP = 8
 SPAN = 4
-CHUNKS = (1, 1, 1, 1, 1, 1, 1, 1)
+UNITS = PARTS
+RELAYS = tuple((u, h, TILES // 2) for u in range(UNITS) for h in (0, TILES // 2))
+LAG = 4
 
 
 def kernel(
@@ -78,9 +80,9 @@
     z_send,
     z_got,
 ):
-    chunks = len(CHUNKS)
-    own = chunks
-    starts = [sum(CHUNKS[:c]) for c in range(chunks)]
+    units = UNITS
+    relays = len(RELAYS)
+    own = units
     dom = lax.axis_index("dom")
     blk = lax.axis_index("blk")
     low, z = dom // GROUP, dom % GROUP
@@ -154,28 +156,22 @@
     tell = remote(listmsg, list_land, list_send, list_recv, partner)
     tell.start()
 
-    hop1 = [
-        remote(
-            labels.at[:, pl.ds(starts[c], CHUNKS[c])],
-            partner_parts[c],
-            hop1_send.at[c],
-            hop1_recv.at[c],
-            partner,
+    def relay_refs(r):
+        unit, first, count = RELAYS[r]
+        at = pl.ds(first, count)
+        return (
+            labels.at[at, unit],
+            partner_parts[unit].at[at],
+            mirror_parts[unit].at[at],
         )
-        for c in range(chunks)
-    ]
-    hop2 = [
-        remote(
-            partner_parts[c],
-            mirror_parts[c],
-            hop2_send.at[c],
-            hop2_recv.at[c],
-            beyond,
-        )
-        for c in range(chunks)
-    ]
-    for c in range(chunks):
-        hop1[c].start()
+
+    hop1, hop2 = [], []
+    for r in range(relays):
+        here, there, far = relay_refs(r)
+        hop1.append(remote(here, there, hop1_send.at[r], hop1_recv.at[r], partner))
+        hop2.append(remote(there, far, hop2_send.at[r], hop2_recv.at[r], beyond))
+    for r in range(relays):
+        hop1[r].start()
 
     others = pl.ds(1, GROUP - 1)
 
@@ -185,8 +181,7 @@
     def z_refs(index, at):
         if index == own:
             return z_stage_own.at[at], z_recv.at[0, at]
-        rows = pl.ds(starts[index], CHUNKS[index])
-        return z_stage[index].at[at], z_recv.at[1, at, rows]
+        return z_stage[index].at[at], z_recv.at[1, at, index]
 
     def x_refs(index, at):
         if index == own:
@@ -215,7 +210,7 @@
         if index == own:
             z_recv[0, 0] = mine
         else:
-            z_recv[1, 0, starts[index] : starts[index] + CHUNKS[index]] = mine
+            z_recv[1, 0, index] = mine
 
     def x_serve(source, which, index):
         stage, recv = (
@@ -248,12 +243,19 @@
         ask(d).wait_recv()
         return carry
 
-    lax.fori_loop(1, GROUP, take_ask, 0)
-    settle = pltpu.make_async_copy(request_land, requests, local_sem.at[0])
-    settle.start()
-    loads[4].wait()
-    settle.wait()
-    x_serve(panel, blk, own)
+    def serve_own_x():
+        lax.fori_loop(1, GROUP, take_ask, 0)
+        settle = pltpu.make_async_copy(request_land, requests, local_sem.at[0])
+        settle.start()
+        loads[4].wait()
+        settle.wait()
+        x_serve(panel, blk, own)
+
+    def hear_list():
+        tell.wait_recv()
+        settle = pltpu.make_async_copy(list_land, partner_list, local_sem.at[1])
+        settle.start()
+        settle.wait()
 
     lane = lax.broadcasted_iota(I32, (GRAIN, 2 * EDGE), 1)
 
@@ -291,8 +293,8 @@
         lax.fori_loop(first, first + count, back, 0)
 
     def sums(weights, row0, row1):
-        tile = lax.broadcasted_iota(I32, (EDGE, 2 * EDGE), 0)
-        wide = lax.broadcasted_iota(I32, (EDGE, 2 * EDGE), 1)
+        tile = lax.broadcasted_iota(I32, (TILES, 2 * EDGE), 0)
+        wide = lax.broadcasted_iota(I32, (TILES, 2 * EDGE), 1)
         chosen = jnp.where(tile == jnp.where(wide < EDGE, row0, row1), 1.0, 0.0)
         return lax.dot_general(
             weights,
@@ -306,7 +308,7 @@
             weights = jnp.concatenate([wi[s, 0], wi[s, 1]], axis=1)
             return value + sums(weights, irows[0, s], irows[1, s])
 
-        start = degree[...] if first else jnp.zeros((EDGE, EDGE), F32)
+        start = degree[...] if first else jnp.zeros((EDGE, TILES), F32)
         degree[...] = lax.fori_loop(first, first + count, one, start)
 
     def cut_degree():
@@ -320,11 +322,8 @@
         degree[...] = lax.fori_loop(0, TILES // 2, one, degree[...])
 
     def set_scale(first, count):
-        used = lax.broadcasted_iota(I32, (EDGE, EDGE), 1) < TILES
-        mask = jnp.concatenate(
-            [seedv[...].astype(F32), jnp.zeros((EDGE - TILES, EDGE), F32)], axis=0
-        ).T
-        factor = jnp.where(mask > 0.5, 0.0, ALPHA / jnp.where(used, degree[...], 1.0))
+        mask = seedv[...].astype(F32).T
+        factor = jnp.where(mask > 0.5, 0.0, ALPHA / degree[...])
         rest = jnp.where(mask > 0.5, 1.0, 1.0 - ALPHA)
         for t in range(first, first + count):
             scale[t] = jnp.broadcast_to(factor[:, t : t + 1], (EDGE, EDGE))
@@ -367,25 +366,19 @@
 
         lax.fori_loop(lo, hi, one, 0)
 
-    def chunk_blocks(c):
-        return [
-            (
-                wm[starts[c] + g],
-                lanes_m[...],
-                x_recv[c][:, :, g].reshape(2 * EDGE, WIDTH),
-            )
-            for g in range(CHUNKS[c])
-        ]
-
-    def mirror_x(cs):
+    def unit_block(u):
+        return (wm[u], lanes_m[...], x_recv[u][...].reshape(2 * EDGE, WIDTH))
+
+    def mirror_x(us, lo, hi):
+        for u in us:
+            x_wait(u)
+
         def one(tg, carry):
-            blocks = []
-            for c in cs:
-                blocks += chunk_blocks(c)
+            blocks = [unit_block(u) for u in us]
             total[row_span(tg), :] += spread_part(tg, blocks)
             return carry
 
-        lax.fori_loop(0, TILES // SPAN, one, 0)
+        lax.fori_loop(lo, hi, one, 0)
 
     def add_cut():
         def one(t, carry):
@@ -401,10 +394,12 @@
 
         lax.fori_loop(0, TILES, one, 0, unroll=2)
 
-    def finish(c):
+    def finish(u):
+        x_wait(u)
+
         def one(tg, carry):
             at = row_span(tg)
-            spread = total[at, :] + spread_part(tg, chunk_blocks(c))
+            spread = total[at, :] + spread_part(tg, [unit_block(u)])
             factor = scale[pl.ds(tg * SPAN, SPAN)].reshape(SPAN * EDGE, EDGE)
             factor = jnp.concatenate([factor, factor], axis=1)
             rest = base[pl.ds(tg * SPAN, SPAN)].reshape(SPAN * EDGE, WIDTH)
@@ -413,45 +408,47 @@
 
         lax.fori_loop(0, TILES // SPAN, one, 0)
 
-    def many(*pieces):
-        def run():
-            for piece in pieces:
-                piece()
-
-        return run
-
-    work = [
-        [(mirror_ids,), (mirror_turn, 0, 4)],
-        [(mirror_turn, 4, 4), (mirror_back, 0, 4)],
-        [(mirror_back, 4, 4), (intra_degree, 0, 16)],
-        [(cut_degree,), (set_scale, 0, 4)],
-        [(set_scale, 4, 12)],
-        [(x_wait, own), (own_x, 0, 4, 0, 4)],
-        [(own_x, 4, 4, 0, 4)],
-        [(x_wait, 0), (x_wait, 1), (x_wait, 2), (x_wait, 3), (mirror_x, [0, 1, 2, 3])],
-        [(x_wait, 4), (x_wait, 5), (mirror_x, [4, 5]), (x_wait, 6), (mirror_x, [6])],
-    ]
-    for c in range(chunks + 1):
-        if c < chunks:
-            hop1[c].wait_recv()
-            hop2[c].start()
-            if c == 0:
-                tell.wait_recv()
-                settle = pltpu.make_async_copy(list_land, partner_list, local_sem.at[1])
-                settle.start()
-                settle.wait()
-            z_serve(partner_parts[c], partner_list, c)
-        if c >= 1:
-            hop2[c - 1].wait_recv()
-            x_serve(mirror_parts[c - 1], other_blk, c - 1)
-        for piece, *given in work[c]:
+    work = {
+        0: [(serve_own_x,)],
+        2: [(mirror_ids,), (mirror_turn, 0, 4)],
+        3: [(mirror_turn, 4, 4)],
+        4: [(mirror_back, 0, 8)],
+        6: [(intra_degree, 0, 8)],
+        7: [(intra_degree, 8, 8)],
+        8: [(cut_degree,)],
+        9: [(set_scale, 0, 4)],
+        10: [(set_scale, 4, 12)],
+        11: [(x_wait, own), (own_x, 0, 4, 0, 1)],
+        12: [(own_x, 0, 4, 1, 3)],
+        13: [(own_x, 0, 4, 3, 4)],
+        14: [(own_x, 4, 4, 0, 2)],
+        15: [(own_x, 4, 4, 2, 3)],
+        16: [(own_x, 4, 4, 3, 4)],
+        17: [(mirror_x, (0, 1, 2), 0, 4)],
+        18: [(mirror_x, (3, 4), 0, 4)],
+    }
+    last = [max(r for r in range(relays) if RELAYS[r][0] == u) for u in range(units)]
+    for r in range(relays + LAG):
+        if r < relays:
+            hop1[r].wait_recv()
+            hop2[r].start()
+            if r == 0:
+                hear_list()
+            if r in last:
+                z_serve(partner_parts[last.index(r)], partner_list, last.index(r))
+        if r >= LAG:
+            hop2[r - LAG].wait_recv()
+            if r - LAG in last:
+                u = last.index(r - LAG)
+                x_serve(mirror_parts[u], other_blk, u)
+        for piece, *given in work.get(r, []):
             piece(*given)
     z_wait(own)
-    for c in range(chunks):
-        z_wait(c)
+    for u in range(units):
+        z_wait(u)
     add_cut()
-    x_wait(chunks - 1)
-    finish(chunks - 1)
+    mirror_x((5, 6), 0, 4)
+    finish(7)
 
     def left(d, carry):
         ask(d).wait_send()
@@ -459,12 +456,12 @@
 
     lax.fori_loop(1, GROUP, left, 0)
     tell.wait_send()
-    for c in range(chunks + 1):
-        z_copy(c, others, 1).wait_send()
-        x_copy(c, others, 1).wait_send()
-    for c in range(chunks):
-        hop1[c].wait_send()
-        hop2[c].wait_send()
+    for u in range(units + 1):
+        z_copy(u, others, 1).wait_send()
+        x_copy(u, others, 1).wait_send()
+    for r in range(relays):
+        hop1[r].wait_send()
+        hop2[r].wait_send()
 
 
 def on_device(
@@ -479,7 +476,8 @@
     cut_slot,
     cut_rows,
 ):
-    chunks = len(CHUNKS)
+    units = UNITS
+    relays = len(RELAYS)
 
     def flat(ids):
         return jnp.swapaxes(ids[0], 0, 1)
@@ -501,10 +499,8 @@
     smem = pltpu.SMEM
     dma = pltpu.SemaphoreType.DMA
 
-    def per_chunk(*shape):
-        return [
-            vmem(tuple(g if n is None else n for n in shape), BF16) for g in CHUNKS
-        ]
+    def per_unit(*shape):
+        return [vmem((*shape, GRAIN, WIDTH), BF16) for _ in range(UNITS)]
 
     scratch = [
         vmem((TILES, PARTS, GRAIN, WIDTH), BF16),
@@ -523,19 +519,19 @@
         vmem((1, TILES), I32),
         smem((GROUP, 2, TILES), I32),
         smem((1, TILES), I32),
-        per_chunk(TILES, None, GRAIN, WIDTH),
-        per_chunk(TILES, None, GRAIN, WIDTH),
+        per_unit(TILES),
+        per_unit(TILES),
         vmem((GROUP, 2, PARTS, GRAIN, WIDTH), BF16),
         vmem((GROUP, 2, PARTS, GRAIN, WIDTH), BF16),
-        per_chunk(GROUP, 2, None, GRAIN, WIDTH),
-        per_chunk(GROUP, 2, None, GRAIN, WIDTH),
+        per_unit(GROUP, 2),
+        per_unit(GROUP, 2),
         vmem((GROUP, PARTS, GRAIN, WIDTH), BF16),
-        per_chunk(GROUP, None, GRAIN, WIDTH),
+        per_unit(GROUP),
         vmem((2, GROUP, PARTS, GRAIN, WIDTH), BF16),
         vmem((PARTS, 2 * EDGE, EDGE), BF16),
         vmem((PARTS, EDGE, 2 * EDGE), BF16),
         vmem((GRAIN, 2 * EDGE), I32),
-        vmem((EDGE, EDGE), F32),
+        vmem((EDGE, TILES), F32),
         vmem((TILES, EDGE, EDGE), F32),
         vmem((TILES, EDGE, WIDTH), F32),
         vmem((TILES * EDGE, WIDTH), F32),
@@ -544,14 +540,14 @@
         dma((GROUP,)),
         dma,
         dma,
-        dma((chunks,)),
-        dma((chunks,)),
-        dma((chunks,)),
-        dma((chunks,)),
-        dma((chunks + 1,)),
-        dma((chunks + 1,)),
-        dma((chunks + 1,)),
-        dma((chunks + 1,)),
+        dma((relays,)),
+        dma((relays,)),
+        dma((relays,)),
+        dma((relays,)),
+        dma((units + 1,)),
+        dma((units + 1,)),
+        dma((units + 1,)),
+        dma((units + 1,)),
     ]
     return pl.pallas_call(
         kernel,

time: 51.3 us -> 47.4 us (0.924)
  Pallas kernels: 50.2 us -> 46.4 us
    pallas_call x1, Pallas kernels: 50.2 us -> 46.4 us  [on_device(): pl.pallas_call(kernel, out_shape=pltpu.VMEM((TILES * EDGE, WIDTH), BF16),...]
where the time goes in v3:
time: 47.4 us; the launch traced here: 47.3 us
  Pallas kernels  46.4 us (98%)
  local copies, waits for them, and re-layouts  0.97 us (2%)
    pallas_call x1, Pallas kernels, on_device(): pl.pallas_call(kernel, out_shape=pltpu.VMEM((TILES * EDGE, WIDTH), BF16),...  46.4 us
    unnamed x1, local copies, waits for them, and re-layouts  0.97 us

profile of v3, /device:TPU:1, one launch (start us, length us, event | category | flops | bytes accessed | tf_op | source)
XLA Modules:
  0.0 47.3 jit_solution(16825817772742485088)
XLA Ops:
  0.0 46.4 %propagate.1 = bf16[2048,256]{1,0:T(8,128)(2,1)S(1)} custom-call(bf16[16,8,16,256]{3,2,1,0:T(8,128)(2,1)} %bitcast.12, bf16[16,128,256]{2,1,0:T(8,128)(2,1)} %bitcast.13, s32[16,128]{1,0:T(8,128)} %bitcast.16, bf16[16,2,128,128]{3,2,1,0:T(8,128)(2,1)} %bitcast.14, bf16[16,128,128]{2,1,0:T(8,128)(2,1)} %bitcast.15, s32[2,16]{1,0:T(2,128)} %bitcast.17, ...), custom_call_target="tpu_custom_call" | custom-call | tf_op jit(solution)/shard_map/propagate/pallas_call | solution.py:552
  46.4 1.0 %copy.12 = bf16[2048,256]{1,0:T(8,128)(2,1)} copy(bf16[2048,256]{1,0:T(8,128)(2,1)S(1)} %propagate.1) | data formatting | bytes 2097152

commit v4 on v3

--- a/solution.py
+++ b/solution.py
@@ -19,7 +19,7 @@
 SPAN = 4
 UNITS = PARTS
 RELAYS = tuple((u, h, TILES // 2) for u in range(UNITS) for h in (0, TILES // 2))
-LAG = 4
+LAG = 3
 
 
 def kernel(
@@ -148,11 +148,14 @@
             colmsg, request_land.at[d], ask_send.at[d], ask_recv.at[d], row_peer(d)
         )
 
-    def start_ask(d, carry):
-        ask(d).start()
+    def spread_order(i):
+        return 1 + (i + 3) % (GROUP - 1)
+
+    def start_ask(i, carry):
+        ask(spread_order(i)).start()
         return carry
 
-    lax.fori_loop(1, GROUP, start_ask, 0)
+    lax.fori_loop(0, GROUP - 1, start_ask, 0)
     tell = remote(listmsg, list_land, list_send, list_recv, partner)
     tell.start()
 
@@ -174,9 +177,6 @@
         hop1[r].start()
 
     others = pl.ds(1, GROUP - 1)
-
-    def spread_order(i):
-        return 1 + (i + 3) % (GROUP - 1)
 
     def z_refs(index, at):
         if index == own:
@@ -392,7 +392,7 @@
             )
             return carry
 
-        lax.fori_loop(0, TILES, one, 0, unroll=2)
+        lax.fori_loop(0, TILES, one, 0, unroll=4)
 
     def finish(u):
         x_wait(u)
@@ -410,22 +410,21 @@
 
     work = {
         0: [(serve_own_x,)],
-        2: [(mirror_ids,), (mirror_turn, 0, 4)],
-        3: [(mirror_turn, 4, 4)],
-        4: [(mirror_back, 0, 8)],
-        6: [(intra_degree, 0, 8)],
-        7: [(intra_degree, 8, 8)],
-        8: [(cut_degree,)],
-        9: [(set_scale, 0, 4)],
-        10: [(set_scale, 4, 12)],
-        11: [(x_wait, own), (own_x, 0, 4, 0, 1)],
-        12: [(own_x, 0, 4, 1, 3)],
-        13: [(own_x, 0, 4, 3, 4)],
-        14: [(own_x, 4, 4, 0, 2)],
-        15: [(own_x, 4, 4, 2, 3)],
-        16: [(own_x, 4, 4, 3, 4)],
-        17: [(mirror_x, (0, 1, 2), 0, 4)],
-        18: [(mirror_x, (3, 4), 0, 4)],
+        2: [(mirror_ids,), (mirror_turn, 0, 2)],
+        3: [(mirror_turn, 2, 2)],
+        4: [(mirror_turn, 4, 4)],
+        5: [(mirror_back, 0, 4)],
+        6: [(mirror_back, 4, 4)],
+        7: [(intra_degree, 0, 8)],
+        8: [(intra_degree, 8, 8)],
+        9: [(cut_degree,)],
+        10: [(set_scale, 0, 8)],
+        11: [(set_scale, 8, 8)],
+        14: [(x_wait, own), (own_x, 0, 4, 0, 1), (own_x, 0, 4, 1, 2)],
+        15: [(own_x, 0, 4, 2, 3), (own_x, 0, 4, 3, 4)],
+        16: [(own_x, 4, 4, 0, 1), (own_x, 4, 4, 1, 2)],
+        17: [(own_x, 4, 4, 2, 3), (own_x, 4, 4, 3, 4)],
+        18: [(mirror_x, (0, 1, 2, 3), 0, 4)],
     }
     last = [max(r for r in range(relays) if RELAYS[r][0] == u) for u in range(units)]
     for r in range(relays + LAG):
@@ -443,11 +442,12 @@
                 x_serve(mirror_parts[u], other_blk, u)
         for piece, *given in work.get(r, []):
             piece(*given)
+    mirror_x((4, 5), 0, 4)
     z_wait(own)
     for u in range(units):
         z_wait(u)
     add_cut()
-    mirror_x((5, 6), 0, 4)
+    mirror_x((6,), 0, 4)
     finish(7)
 
     def left(d, carry):

time: 47.4 us -> 46.5 us (0.981)
  Pallas kernels: 46.4 us -> 45.5 us
    pallas_call x1, Pallas kernels: 46.4 us -> 45.5 us  [on_device(): pl.pallas_call(kernel, out_shape=pltpu.VMEM((TILES * EDGE, WIDTH), BF16),...]
where the time goes in v4:
time: 46.5 us
  Pallas kernels  45.5 us (98%)
  local copies, waits for them, and re-layouts  0.97 us (2%)
    pallas_call x1, Pallas kernels, on_device(): pl.pallas_call(kernel, out_shape=pltpu.VMEM((TILES * EDGE, WIDTH), BF16),...  45.5 us
    unnamed x1, local copies, waits for them, and re-layouts  0.97 us

profile of v4, /device:TPU:1, one launch (start us, length us, event | category | flops | bytes accessed | tf_op | source)
XLA Modules:
  0.0 46.5 jit_solution(835126200276967081)
XLA Ops:
  0.0 45.5 %propagate.1 = bf16[2048,256]{1,0:T(8,128)(2,1)S(1)} custom-call(bf16[16,8,16,256]{3,2,1,0:T(8,128)(2,1)} %bitcast.12, bf16[16,128,256]{2,1,0:T(8,128)(2,1)} %bitcast.13, s32[16,128]{1,0:T(8,128)} %bitcast.16, bf16[16,2,128,128]{3,2,1,0:T(8,128)(2,1)} %bitcast.14, bf16[16,128,128]{2,1,0:T(8,128)(2,1)} %bitcast.15, s32[2,16]{1,0:T(2,128)} %bitcast.17, ...), custom_call_target="tpu_custom_call" | custom-call | tf_op jit(solution)/shard_map/propagate/pallas_call | solution.py:552
  45.5 1.0 %copy.12 = bf16[2048,256]{1,0:T(8,128)(2,1)} copy(bf16[2048,256]{1,0:T(8,128)(2,1)S(1)} %propagate.1) | data formatting | bytes 2097152

commit v5 on v4

--- a/solution.py
+++ b/solution.py
@@ -145,7 +145,7 @@
 
     def ask(d):
         return remote(
-            colmsg, request_land.at[d], ask_send.at[d], ask_recv.at[d], row_peer(d)
+            colmsg, request_land.at[d], ask_send, ask_recv, row_peer(d)
         )
 
     def spread_order(i):
@@ -171,8 +171,8 @@
     hop1, hop2 = [], []
     for r in range(relays):
         here, there, far = relay_refs(r)
-        hop1.append(remote(here, there, hop1_send.at[r], hop1_recv.at[r], partner))
-        hop2.append(remote(there, far, hop2_send.at[r], hop2_recv.at[r], beyond))
+        hop1.append(remote(here, there, hop1_send, hop1_recv.at[r], partner))
+        hop2.append(remote(there, far, hop2_send, hop2_recv.at[r], beyond))
     for r in range(relays):
         hop1[r].start()
 
@@ -239,12 +239,12 @@
     loads[3].wait()
     z_serve(panel, slist, own)
 
-    def take_ask(d, carry):
-        ask(d).wait_recv()
-        return carry
+    def all_asks():
+        landed = request_land.at[others]
+        return remote(landed, landed, ask_send, ask_recv, row_peer(1))
 
     def serve_own_x():
-        lax.fori_loop(1, GROUP, take_ask, 0)
+        all_asks().wait_recv()
         settle = pltpu.make_async_copy(request_land, requests, local_sem.at[0])
         settle.start()
         loads[4].wait()
@@ -450,18 +450,13 @@
     mirror_x((6,), 0, 4)
     finish(7)
 
-    def left(d, carry):
-        ask(d).wait_send()
-        return carry
-
-    lax.fori_loop(1, GROUP, left, 0)
+    all_asks().wait_send()
     tell.wait_send()
     for u in range(units + 1):
         z_copy(u, others, 1).wait_send()
         x_copy(u, others, 1).wait_send()
-    for r in range(relays):
-        hop1[r].wait_send()
-        hop2[r].wait_send()
+    remote(labels, panel, hop1_send, hop1_recv.at[0], partner).wait_send()
+    remote(panel, panel, hop2_send, hop2_recv.at[0], beyond).wait_send()
 
 
 def on_device(
@@ -536,13 +531,13 @@
         vmem((TILES, EDGE, WIDTH), F32),
         vmem((TILES * EDGE, WIDTH), F32),
         dma((12,)),
-        dma((GROUP,)),
-        dma((GROUP,)),
+        dma,
+        dma,
+        dma,
         dma,
         dma,
         dma((relays,)),
-        dma((relays,)),
-        dma((relays,)),
+        dma,
         dma((relays,)),
         dma((units + 1,)),
         dma((units + 1,)),

time: 46.5 us -> 46.1 us (level)
  Pallas kernels: 45.5 us -> 45 us
    pallas_call x1, Pallas kernels: 45.5 us -> 45 us  [on_device(): pl.pallas_call(kernel, out_shape=pltpu.VMEM((TILES * EDGE, WIDTH), BF16),...]
where the time goes in v5:
time: 46.1 us; the launch traced here: 46 us
  Pallas kernels  45 us (98%)
  local copies, waits for them, and re-layouts  0.97 us (2%)
    pallas_call x1, Pallas kernels, on_device(): pl.pallas_call(kernel, out_shape=pltpu.VMEM((TILES * EDGE, WIDTH), BF16),...  45 us
    unnamed x1, local copies, waits for them, and re-layouts  0.97 us

profile of v5, /device:TPU:1, one launch (start us, length us, event | category | flops | bytes accessed | tf_op | source)
XLA Modules:
  0.0 46.0 jit_solution(5421245750975565428)
XLA Ops:
  0.0 45.0 %propagate.1 = bf16[2048,256]{1,0:T(8,128)(2,1)S(1)} custom-call(bf16[16,8,16,256]{3,2,1,0:T(8,128)(2,1)} %bitcast.12, bf16[16,128,256]{2,1,0:T(8,128)(2,1)} %bitcast.13, s32[16,128]{1,0:T(8,128)} %bitcast.16, bf16[16,2,128,128]{3,2,1,0:T(8,128)(2,1)} %bitcast.14, bf16[16,128,128]{2,1,0:T(8,128)(2,1)} %bitcast.15, s32[2,16]{1,0:T(2,128)} %bitcast.17, ...), custom_call_target="tpu_custom_call" | custom-call | tf_op jit(solution)/shard_map/propagate/pallas_call | solution.py:547
  45.0 1.0 %copy.12 = bf16[2048,256]{1,0:T(8,128)(2,1)} copy(bf16[2048,256]{1,0:T(8,128)(2,1)S(1)} %propagate.1) | data formatting | bytes 2097152

commit v6 on v5

--- a/solution.py
+++ b/solution.py
@@ -190,11 +190,11 @@
 
     def z_copy(index, at, d):
         src, dst = z_refs(index, at)
-        return remote(src, dst, z_send.at[index], z_got.at[index], z_peer(d))
+        return remote(src, dst, z_send, z_got.at[index], z_peer(d))
 
     def x_copy(index, at, d):
         src, dst = x_refs(index, at)
-        return remote(src, dst, x_send.at[index], x_got.at[index], row_peer(d))
+        return remote(src, dst, x_send, x_got.at[index], row_peer(d))
 
     def z_serve(source, wanted, index):
         stage = z_stage_own if index == own else z_stage[index]
@@ -452,9 +452,10 @@
 
     all_asks().wait_send()
     tell.wait_send()
-    for u in range(units + 1):
-        z_copy(u, others, 1).wait_send()
-        x_copy(u, others, 1).wait_send()
+    sent_z = x_stage_own.at[others]
+    sent_x = base.at[pl.ds(0, 2 * GROUP - 2)]
+    remote(sent_z, sent_z, z_send, z_got.at[0], z_peer(1)).wait_send()
+    remote(sent_x, sent_x, x_send, x_got.at[0], row_peer(1)).wait_send()
     remote(labels, panel, hop1_send, hop1_recv.at[0], partner).wait_send()
     remote(panel, panel, hop2_send, hop2_recv.at[0], beyond).wait_send()
 
@@ -539,9 +540,9 @@
         dma((relays,)),
         dma,
         dma((relays,)),
+        dma,
         dma((units + 1,)),
-        dma((units + 1,)),
-        dma((units + 1,)),
+        dma,
         dma((units + 1,)),
     ]
     return pl.pallas_call(

time: 46.1 us -> 45.9 us (level)
  no operation moved by 1% of the time
where the time goes in v6:
time: 45.9 us; the launch traced here: 45.8 us
  Pallas kernels  44.8 us (98%)
  local copies, waits for them, and re-layouts  0.97 us (2%)
    pallas_call x1, Pallas kernels, on_device(): pl.pallas_call(kernel, out_shape=pltpu.VMEM((TILES * EDGE, WIDTH), BF16),...  44.8 us
    unnamed x1, local copies, waits for them, and re-layouts  0.97 us

profile of v6, /device:TPU:1, one launch (start us, length us, event | category | flops | bytes accessed | tf_op | source)
XLA Modules:
  0.0 45.8 jit_solution(17246009486048602338)
XLA Ops:
  0.0 44.8 %propagate.1 = bf16[2048,256]{1,0:T(8,128)(2,1)S(1)} custom-call(bf16[16,8,16,256]{3,2,1,0:T(8,128)(2,1)} %bitcast.12, bf16[16,128,256]{2,1,0:T(8,128)(2,1)} %bitcast.13, s32[16,128]{1,0:T(8,128)} %bitcast.16, bf16[16,2,128,128]{3,2,1,0:T(8,128)(2,1)} %bitcast.14, bf16[16,128,128]{2,1,0:T(8,128)(2,1)} %bitcast.15, s32[2,16]{1,0:T(2,128)} %bitcast.17, ...), custom_call_target="tpu_custom_call" | custom-call | tf_op jit(solution)/shard_map/propagate/pallas_call | solution.py:548
  44.9 1.0 %copy.12 = bf16[2048,256]{1,0:T(8,128)(2,1)} copy(bf16[2048,256]{1,0:T(8,128)(2,1)S(1)} %propagate.1) | data formatting | bytes 2097152
